TPU v7x, 32 devices: a whole 2x2x4 slice. The times are simulated.
32 devices in a mesh: dp: 16 (over z, x, core), mp: 2 (over y).
Axes of the slice: x: 2, y: 2, z: 4, core: 2. Of those that a mesh axis runs over, the one named last changes fastest.
Arguments:
- tokens: bfloat16 [32768, 1024], P(('dp', 'mp')), may hold values from -6 to 6
- first_values: bfloat16 [32768, 1024], P('dp', 'mp'), may hold values from -6 to 6
- lengths: int32 [16], P('dp'), may hold values from 128 to 2048, as said below
- cotangent: bfloat16 [32768, 1024], P(('dp', 'mp')), may hold values from -6 to 6
- w_qkv: float32 [1024, 3, 1024], P(None, None, 'mp'), may hold values from -0.1875 to 0.1875
- w_out: float32 [1024, 1024], P('mp'), may hold values from -4 to 4
- w_gateup: float32 [1024, 2, 2816], P(None, None, 'mp'), may hold values from -0.1875 to 0.1875
- w_down: float32 [2816, 1024], P('mp'), may hold values from -0.109375 to 0.109375
- gains: float32 [2, 1024], replicated, may hold values from 0.4 to 1.8
- moment_qkv: float32 [1024, 3, 1024], P('dp', None, 'mp'), may hold values from -3 to 3
- moment_out: float32 [1024, 1024], P('mp', 'dp'), may hold values from -0.15625 to 0.15625
- moment_gateup: float32 [1024, 2, 2816], P('dp', None, 'mp'), may hold values from -1.25 to 1.25
- moment_down: float32 [2816, 1024], P('mp', 'dp'), may hold values from -2.5 to 2.5
- moment_gains: float32 [2, 1024], replicated, may hold values from -2.5 to 2.5
- average_qkv: float32 [1024, 3, 1024], P('dp', None, 'mp'), may hold values from -0.1875 to 0.1875
- average_out: float32 [1024, 1024], P('mp', 'dp'), may hold values from -12 to 12
- average_gateup: float32 [1024, 2, 2816], P('dp', None, 'mp'), may hold values from -0.1875 to 0.1875
- average_down: float32 [2816, 1024], P('mp', 'dp'), may hold values from -0.109375 to 0.109375
- average_gains: float32 [2, 1024], replicated, may hold values from 0.5 to 1.5
Outputs:
- output: bfloat16 [32768, 1024], P(('dp', 'mp'))
- input_grad: float32 [32768, 1024], P(('dp', 'mp'))
- first_values_grad: float32 [32768, 1024], P('dp', 'mp')
- qkv_grad: float32 [1024, 3, 1024], P('dp', None, 'mp')
- qkv_moment: float32 [1024, 3, 1024], P('dp', None, 'mp')
- qkv_average: float32 [1024, 3, 1024], P('dp', None, 'mp')
- qkv_weight: float32 [1024, 3, 1024], P('dp', None, 'mp')
- out_grad: float32 [1024, 1024], P('mp', 'dp')
- out_moment: float32 [1024, 1024], P('mp', 'dp')
- out_average: float32 [1024, 1024], P('mp', 'dp')
- out_weight: float32 [1024, 1024], P('mp', 'dp')
- gateup_grad: float32 [1024, 2, 2816], P('dp', None, 'mp')
- gateup_moment: float32 [1024, 2, 2816], P('dp', None, 'mp')
- gateup_average: float32 [1024, 2, 2816], P('dp', None, 'mp')
- gateup_weight: float32 [1024, 2, 2816], P('dp', None, 'mp')
- down_grad: float32 [2816, 1024], P('mp', 'dp')
- down_moment: float32 [2816, 1024], P('mp', 'dp')
- down_average: float32 [2816, 1024], P('mp', 'dp')
- down_weight: float32 [2816, 1024], P('mp', 'dp')
- gains_grad: float32 [2, 1024], replicated
- gains_moment: float32 [2, 1024], replicated
- gains_average: float32 [2, 1024], replicated
- gains_new: float32 [2, 1024], replicated
Inputs may be any that keep to these rules, and one draw needn't show every extreme that they name: `lengths`: valid tokens of each of the 16 slots; some slot holds 2048 and some holds exactly 128.
All inputs are finite; a program needn't handle non-finite values.
Results may differ from a plain program's by a relative error of at most 0.014.
Values may be sent and summed in bfloat16 or wider, within the bound.
No kernel may reach another device: no remote copies, remote signals or barrier semaphores. Data moves between devices by JAX's collectives and lax.ppermute only.
A program may use at most 320 MiB of HBM per device.

v0:
```python
import math

import jax
import jax.numpy as jnp
from jax import lax
from jax.sharding import PartitionSpec as P

HEAD_DIM = 64


EPS = 1e-06
NEG_BIG = -1e30
HALF = 0.5
MOMENTUM = 0.5
AVERAGE_DECAY = 0.5
RATE_QKV = 0.05
RATE_OUT = 20.0
RATE_GATEUP = 0.12
RATE_DOWN = 0.04
RATE_GAINS = 0.6


def normalize(values, gain):
    inverse = lax.rsqrt(jnp.mean(values * values, axis=-1, keepdims=True) + EPS)
    unit = values * inverse
    return (unit * gain, unit, inverse)


def norm_back(grad_norm, gain, unit, inverse):
    scaled = grad_norm * gain
    return inverse * (scaled - unit * jnp.mean(scaled * unit, axis=-1, keepdims=True))


def rope_tables(length, head_size):
    half_size = head_size // 2
    freqs = jnp.power(10000.0, -2.0 * jnp.arange(half_size, dtype=jnp.float32) / head_size)
    angles = jnp.arange(length, dtype=jnp.float32)[:, None] * freqs[None, :]
    return (jnp.cos(angles)[:, None, :], jnp.sin(angles)[:, None, :])


def rotate(values, cosine, sine):
    half_size = values.shape[-1] // 2
    first_half = values[..., :half_size]
    second_half = values[..., half_size:]
    return jnp.concatenate(
        [first_half * cosine - second_half * sine, second_half * cosine + first_half * sine],
        axis=-1,
    )


def unrotate(grads, cosine, sine):
    half_size = grads.shape[-1] // 2
    first_half = grads[..., :half_size]
    second_half = grads[..., half_size:]
    return jnp.concatenate(
        [first_half * cosine + second_half * sine, second_half * cosine - first_half * sine],
        axis=-1,
    )


def dot_last(left, right):
    return lax.dot_general(
        left, right, (((1,), (1,)), ((), ())), preferred_element_type=jnp.float32
    )


def dot_first(left, right):
    return lax.dot_general(
        left, right, (((0,), (0,)), ((), ())), preferred_element_type=jnp.float32
    )


def block_scores(query_block, keys, start, length, scale):
    block_len = query_block.shape[0]
    key_len = keys.shape[0]
    scores = (
        jnp.einsum("qhd,khd->hqk", query_block, keys, preferred_element_type=jnp.float32) * scale
    )
    query_pos = start + jnp.arange(block_len, dtype=jnp.int32)
    key_pos = jnp.arange(key_len, dtype=jnp.int32)
    allowed = (key_pos[None, :] <= query_pos[:, None]) & (key_pos[None, :] < length)
    return jnp.where(allowed[None], scores, NEG_BIG)


def attend_forward(queries, keys, values, lengths):
    slot_count, slot_len, heads_here, head_size = queries.shape
    block_len = min(512, slot_len)
    blocks = slot_len // block_len
    scale = 1.0 / math.sqrt(head_size)
    starts = jnp.arange(blocks, dtype=jnp.int32) * block_len

    def per_slot(item):
        slot_queries, slot_keys, slot_values, length = item

        def per_block(inner):
            query_block, start = inner
            scores = block_scores(query_block, slot_keys, start, length, scale)
            peak = jnp.max(scores, axis=-1, keepdims=True)
            raw_weights = jnp.exp(scores - peak)
            total = jnp.sum(raw_weights, axis=-1, keepdims=True)
            probs = raw_weights / total
            mixed = jnp.einsum(
                "hqk,khd->qhd",
                probs.astype(jnp.bfloat16),
                slot_values,
                preferred_element_type=jnp.float32,
            )
            return (mixed, (peak + jnp.log(total))[..., 0])

        mixed, log_totals = lax.map(
            per_block, (slot_queries.reshape(blocks, block_len, heads_here, head_size), starts)
        )
        return (mixed.reshape(slot_len, heads_here, head_size), log_totals)

    return lax.map(per_slot, (queries, keys, values, lengths))


def attend_backward(queries, keys, values, lengths, grad_mixed, log_totals):
    slot_count, slot_len, heads_here, head_size = queries.shape
    block_len = min(512, slot_len)
    blocks = slot_len // block_len
    scale = 1.0 / math.sqrt(head_size)
    starts = jnp.arange(blocks, dtype=jnp.int32) * block_len

    def per_slot(item):
        slot_queries, slot_keys, slot_values, length, slot_grads, slot_totals = item

        def per_block(carry, inner):
            key_grad, value_grad = carry
            query_block, grad_block, total_block, start = inner
            scores = block_scores(query_block, slot_keys, start, length, scale)
            probs = jnp.exp(scores - total_block[..., None])
            prob_grad = jnp.einsum(
                "qhd,khd->hqk", grad_block, slot_values, preferred_element_type=jnp.float32
            )
            center = jnp.sum(probs * prob_grad, axis=-1, keepdims=True)
            score_grad = (probs * (prob_grad - center)).astype(jnp.bfloat16)
            query_grad = (
                jnp.einsum(
                    "hqk,khd->qhd", score_grad, slot_keys, preferred_element_type=jnp.float32
                )
                * scale
            )
            key_grad = (
                key_grad
                + jnp.einsum(
                    "hqk,qhd->khd", score_grad, query_block, preferred_element_type=jnp.float32
                )
                * scale
            )
            value_grad = value_grad + jnp.einsum(
                "hqk,qhd->khd",
                probs.astype(jnp.bfloat16),
                grad_block,
                preferred_element_type=jnp.float32,
            )
            return ((key_grad, value_grad), query_grad)

        empty = jnp.zeros((slot_len, heads_here, head_size), jnp.float32)
        shaped_queries = slot_queries.reshape(blocks, block_len, heads_here, head_size)
        shaped_grads = slot_grads.reshape(blocks, block_len, heads_here, head_size)
        (key_grad, value_grad), query_grad = lax.scan(
            per_block, (empty, empty), (shaped_queries, shaped_grads, slot_totals, starts)
        )
        return (query_grad.reshape(slot_len, heads_here, head_size), key_grad, value_grad)

    return lax.map(per_slot, (queries, keys, values, lengths, grad_mixed, log_totals))


def row_valid(lengths, slot_len, start, count):
    index = start + jnp.arange(count, dtype=jnp.int32)
    slot_of = index // slot_len
    place = index % slot_len
    slot_ids = jnp.arange(lengths.shape[0], dtype=jnp.int32)
    limit = jnp.sum(jnp.where(slot_of[:, None] == slot_ids[None, :], lengths[None, :], 0), axis=1)
    return (place < limit).astype(jnp.float32)


def nesterov(grad, weight, moment, average, rate):
    moment_new = MOMENTUM * moment + grad
    weight_new = weight - rate * (grad + MOMENTUM * moment_new)
    average_new = AVERAGE_DECAY * average + (1.0 - AVERAGE_DECAY) * weight_new
    return (grad, moment_new, average_new, weight_new)


def shards(
    tokens,
    first_values,
    lengths,
    cotangent,
    w_qkv,
    w_out,
    w_gateup,
    w_down,
    gains,
    moment_qkv,
    moment_out,
    moment_gateup,
    moment_down,
    moment_gains,
    average_qkv,
    average_out,
    average_gateup,
    average_down,
    average_gains,
):
    local_rows, model = tokens.shape
    mp_count = lax.axis_size("mp")
    dp_count = lax.axis_size("dp")
    mp_index = lax.axis_index("mp")
    dp_index = lax.axis_index("dp")
    slot_count = lengths.shape[0]
    group_rows = local_rows * mp_count
    slot_len = group_rows // slot_count
    head_cols = w_qkv.shape[2]
    hidden_cols = w_gateup.shape[2]
    heads_here = head_cols // HEAD_DIM
    row_start = mp_index * local_rows
    all_tokens = group_rows * dp_count
    root_count = math.sqrt(all_tokens)
    qkv_bf = w_qkv.astype(jnp.bfloat16).reshape(model, 3 * head_cols)
    out_bf = w_out.astype(jnp.bfloat16)
    gateup_bf = w_gateup.astype(jnp.bfloat16).reshape(model, 2 * hidden_cols)
    down_bf = w_down.astype(jnp.bfloat16)
    gain_one = gains[0]
    gain_two = gains[1]
    valid_local = row_valid(lengths, slot_len, row_start, local_rows)
    x_local = tokens.astype(jnp.float32)
    x_group = lax.all_gather(tokens, "mp", axis=0, tiled=True).astype(jnp.float32)
    norm_one, unit_one, inverse_one = normalize(x_group, gain_one)
    norm_one_bf = norm_one.astype(jnp.bfloat16)
    qkv = jnp.dot(norm_one_bf, qkv_bf, preferred_element_type=jnp.float32)
    qkv = qkv.reshape(slot_count, slot_len, 3, heads_here, HEAD_DIM)
    cosine, sine = rope_tables(slot_len, HEAD_DIM)
    queries = rotate(qkv[:, :, 0], cosine, sine).astype(jnp.bfloat16)
    keys = rotate(qkv[:, :, 1], cosine, sine).astype(jnp.bfloat16)
    first_shaped = first_values.astype(jnp.float32).reshape(
        slot_count, slot_len, heads_here, HEAD_DIM
    )
    values = (HALF * qkv[:, :, 2] + HALF * first_shaped).astype(jnp.bfloat16)
    mixed, log_totals = attend_forward(queries, keys, values, lengths)
    mixed_bf = mixed.reshape(group_rows, head_cols).astype(jnp.bfloat16)
    resid_local = x_local + lax.psum_scatter(
        jnp.dot(mixed_bf, out_bf, preferred_element_type=jnp.float32),
        "mp",
        scatter_dimension=0,
        tiled=True,
    )
    norm_two_local, unit_two, inverse_two = normalize(resid_local, gain_two)
    norm_two_bf = lax.all_gather(norm_two_local.astype(jnp.bfloat16), "mp", axis=0, tiled=True)
    gateup = jnp.dot(norm_two_bf, gateup_bf, preferred_element_type=jnp.float32)
    gate_val = gateup[:, :hidden_cols]
    up_val = gateup[:, hidden_cols:]
    sigmoid_gate = jax.nn.sigmoid(gate_val)
    silu_gate = gate_val * sigmoid_gate
    hidden_bf = (silu_gate * up_val).astype(jnp.bfloat16)
    result_local = resid_local + lax.psum_scatter(
        jnp.dot(hidden_bf, down_bf, preferred_element_type=jnp.float32),
        "mp",
        scatter_dimension=0,
        tiled=True,
    )
    output = result_local.astype(jnp.bfloat16)
    grad_local = (cotangent.astype(jnp.float32) * valid_local[:, None]).astype(jnp.bfloat16)
    grad_group = lax.all_gather(grad_local, "mp", axis=0, tiled=True)
    grad_down = dot_first(hidden_bf, grad_group)
    grad_hidden = dot_last(grad_group, down_bf)
    grad_gate = grad_hidden * up_val * sigmoid_gate * (1.0 + gate_val * (1.0 - sigmoid_gate))
    grad_up = grad_hidden * silu_gate
    grad_gateup_bf = jnp.concatenate([grad_gate, grad_up], axis=1).astype(jnp.bfloat16)
    grad_gateup = dot_first(norm_two_bf, grad_gateup_bf)
    grad_norm_two = lax.psum_scatter(
        dot_last(grad_gateup_bf, gateup_bf), "mp", scatter_dimension=0, tiled=True
    )
    grad_resid_local = grad_local.astype(jnp.float32) + norm_back(
        grad_norm_two, gain_two, unit_two, inverse_two
    )
    gain_two_grad = jnp.sum(grad_norm_two * unit_two, axis=0)
    grad_resid_bf = lax.all_gather(grad_resid_local.astype(jnp.bfloat16), "mp", axis=0, tiled=True)
    grad_out = dot_first(mixed_bf, grad_resid_bf)
    grad_mixed = dot_last(grad_resid_bf, out_bf).astype(jnp.bfloat16)
    grad_mixed = grad_mixed.reshape(slot_count, slot_len, heads_here, HEAD_DIM)
    query_grad, key_grad, value_grad = attend_backward(
        queries, keys, values, lengths, grad_mixed, log_totals
    )
    first_values_grad = (HALF * value_grad).reshape(group_rows, head_cols)
    grad_qkv_bf = jnp.stack(
        [unrotate(query_grad, cosine, sine), unrotate(key_grad, cosine, sine), HALF * value_grad],
        axis=2,
    )
    grad_qkv_bf = grad_qkv_bf.reshape(group_rows, 3 * head_cols).astype(jnp.bfloat16)
    grad_qkv = dot_first(norm_one_bf, grad_qkv_bf)
    unit_local = lax.dynamic_slice_in_dim(unit_one, row_start, local_rows, 0)
    inverse_local = lax.dynamic_slice_in_dim(inverse_one, row_start, local_rows, 0)
    grad_norm_one = lax.psum_scatter(
        dot_last(grad_qkv_bf, qkv_bf).astype(jnp.bfloat16), "mp", scatter_dimension=0, tiled=True
    ).astype(jnp.float32)
    input_grad = grad_resid_local + norm_back(grad_norm_one, gain_one, unit_local, inverse_local)
    gain_one_grad = jnp.sum(grad_norm_one * unit_local, axis=0)
    sum_qkv, sum_out, sum_gateup, sum_down = (
        lax.psum_scatter(
            grad_qkv.reshape(model, 3, head_cols), "dp", scatter_dimension=0, tiled=True
        ),
        lax.psum_scatter(grad_out, "dp", scatter_dimension=1, tiled=True),
        lax.psum_scatter(
            grad_gateup.reshape(model, 2, hidden_cols), "dp", scatter_dimension=0, tiled=True
        ),
        lax.psum_scatter(grad_down, "dp", scatter_dimension=1, tiled=True),
    )
    gain_sum = lax.psum(jnp.stack([gain_one_grad, gain_two_grad], axis=0), ("dp", "mp"))
    share = model // dp_count
    own_qkv = lax.dynamic_slice_in_dim(w_qkv, dp_index * share, share, 0)
    own_out = lax.dynamic_slice_in_dim(w_out, dp_index * share, share, 1)
    own_gateup = lax.dynamic_slice_in_dim(w_gateup, dp_index * share, share, 0)
    own_down = lax.dynamic_slice_in_dim(w_down, dp_index * share, share, 1)
    qkv_set = nesterov(sum_qkv / root_count, own_qkv, moment_qkv, average_qkv, RATE_QKV)
    out_set = nesterov(sum_out / root_count, own_out, moment_out, average_out, RATE_OUT)
    gateup_set = nesterov(
        sum_gateup / root_count, own_gateup, moment_gateup, average_gateup, RATE_GATEUP
    )
    down_set = nesterov(sum_down / root_count, own_down, moment_down, average_down, RATE_DOWN)
    gains_set = nesterov(gain_sum / root_count, gains, moment_gains, average_gains, RATE_GAINS)
    return (
        output,
        input_grad,
        first_values_grad,
        qkv_set[0],
        qkv_set[1],
        qkv_set[2],
        qkv_set[3],
        out_set[0],
        out_set[1],
        out_set[2],
        out_set[3],
        gateup_set[0],
        gateup_set[1],
        gateup_set[2],
        gateup_set[3],
        down_set[0],
        down_set[1],
        down_set[2],
        down_set[3],
        gains_set[0],
        gains_set[1],
        gains_set[2],
        gains_set[3],
    )


def solution(mesh):
    placed = (
        P(("dp", "mp"), None),
        P("dp", "mp"),
        P("dp"),
        P(("dp", "mp"), None),
        P(None, None, "mp"),
        P("mp", None),
        P(None, None, "mp"),
        P("mp", None),
        P(),
        P("dp", None, "mp"),
        P("mp", "dp"),
        P("dp", None, "mp"),
        P("mp", "dp"),
        P(),
        P("dp", None, "mp"),
        P("mp", "dp"),
        P("dp", None, "mp"),
        P("mp", "dp"),
        P(),
    )
    return jax.shard_map(
        shards,
        mesh=mesh,
        in_specs=placed,
        out_specs=(
            P(("dp", "mp"), None),
            P(("dp", "mp"), None),
            P("dp", "mp"),
            P("dp", None, "mp"),
            P("dp", None, "mp"),
            P("dp", None, "mp"),
            P("dp", None, "mp"),
            P("mp", "dp"),
            P("mp", "dp"),
            P("mp", "dp"),
            P("mp", "dp"),
            P("dp", None, "mp"),
            P("dp", None, "mp"),
            P("dp", None, "mp"),
            P("dp", None, "mp"),
            P("mp", "dp"),
            P("mp", "dp"),
            P("mp", "dp"),
            P("mp", "dp"),
            P(),
            P(),
            P(),
            P(),
        ),
        check_vma=False,
    )
```

profile of v0, /device:TPU:0, one launch (start us, length us, event | category | flops | bytes accessed | tf_op | source)
XLA Modules:
  0.0 1614.2 jit_solution(7207916542370166437)
XLA Ops:
  19.2 49.9 %all-gather.5.cloned.1.call-done = bf16[2048,1024]{1,0:T(8,128)(2,1)} async-done(((bf16[1024,1024]{1,0:T(8,128)(2,1)}), bf16[2048,1024]{1,0:T(8,128)(2,1)}) %all-gather.5.cloned.1.call-update) | async-done | bytes 4194320 | tf_op jit(solution)/shard_map/all_gather | solution.py:229
  102.1 194.5 %while.47 = (s32[]{:T(128)}, bf16[4,512,8,64]{1,3,2,0:T(8,128)(2,1)}, f32[4,8,512]{2,1,0:T(8,128)}, s32[4]{0:T(128)S(1)}, s32[]{:T(128)}, /*index=5*/bf16[4,512,...) while((s32[]{:T(128)}, ...), condition=%wide.region_4.5_spmd, body=%wide.region_1.4_spmd.sunk | while | flops 2250242560 | bytes 110764160 | solution.py:110
  308.8 98.9 %reduce-scatter.8.cloned.1.call-done = f32[1024,1024]{1,0:T(8,128)} async-done(((f32[2048,1024]{1,0:T(8,128)}), f32[1024,1024]{1,0:T(8,128)}) %reduce-scatter.8.cloned.1.call-update) | async-done | bytes 4194320 | tf_op jit(solution)/shard_map/reduce_scatter | solution.py:243
  427.8 43.4 %all-gather.7.cloned.1.call-done = bf16[2048,1024]{1,0:T(8,128)(2,1)} async-done(((bf16[1024,1024]{1,0:T(8,128)(2,1)}), bf16[2048,1024]{1,0:T(8,128)(2,1)}) %all-gather.7.cloned.1.call-update) | async-done | bytes 4194320 | tf_op jit(solution)/shard_map/all_gather | solution.py:250
  471.2 19.8 %fusion.71 = f32[2048,2816]{1,0:T(8,128)} fusion(bf16[2048,1024]{1,0:T(8,128)(2,1)} %all-gather.7.cloned.1.call-done, bf16[1024,2816]{1,0:T(8,128)(2,1)} %bitcast.178), kind=kOutput, calls=%fused_computation.162 | convolution fusion | flops 11811160064 | bytes 33030144 | tf_op jit(solution)/shard_map/dot_general | solution.py:251
  490.9 39.1 %all-gather.9.cloned.1.call-done = bf16[2048,1024]{1,0:T(8,128)(2,1)} async-done(((bf16[1024,1024]{1,0:T(8,128)(2,1)}), bf16[2048,1024]{1,0:T(8,128)(2,1)}) %all-gather.9.cloned.1.call-update) | async-done | bytes 4194320 | tf_op jit(solution)/shard_map/all_gather | solution.py:265
  530.0 22.1 %multiply_convert_fusion.2 = (bf16[2048,1408]{1,0:T(8,128)(2,1)}, bf16[2048,1408]{1,0:T(8,128)(2,1)}, bf16[2048,1408]{1,0:T(8,128)(2,1)}) fusion(f32[2048,2816]{1,0:T(8,128)} %fusion.71, bf16[2048,1024]{1,0:T(8,128)(2,1)} %all-gather.9.cloned.1.call-done, f32[1408,1024]{1,0:T(8,128)} %param.30), kind=kOutput, calls=%fused_computation.49 | convolution fusion | flops 5950275584 | bytes 50331648 | tf_op jit(solution)/shard_map/dot_general | solution.py:62
  552.1 18.2 %fusion.34 = f32[2048,1024]{1,0:T(8,128)} fusion(bf16[1024,2816]{1,0:T(8,128)(2,1)} %bitcast.179, bf16[2048,1408]{1,0:T(8,128)(2,1)} %get-tuple-element.394, bf16[2048,1408]{1,0:T(8,128)(2,1)} %get-tuple-element.393), kind=kOutput, calls=%fused_computation.58 | convolution fusion | flops 11834228736 | bytes 25690112 | tf_op jit(solution)/shard_map/dot_general | solution.py:62
  570.3 99.3 %reduce-scatter.12.cloned.1.call-done = f32[1024,1024]{1,0:T(8,128)} async-done(((f32[2048,1024]{1,0:T(8,128)}), f32[1024,1024]{1,0:T(8,128)}) %reduce-scatter.12.cloned.1.call-update) | async-done | bytes 4194320 | tf_op jit(solution)/shard_map/reduce_scatter | solution.py:272
  678.3 19.8 %fusion.33 = f32[1024,2816]{1,0:T(8,128)} fusion(bf16[2048,1024]{1,0:T(8,128)(2,1)} %all-gather.7.cloned.1.call-done, bf16[2048,1408]{1,0:T(8,128)(2,1)} %get-tuple-element.394, bf16[2048,1408]{1,0:T(8,128)(2,1)} %get-tuple-element.393), kind=kOutput, calls=%fused_computation.57 | convolution fusion | flops 11834228736 | bytes 27262976 | tf_op jit(solution)/shard_map/dot_general | solution.py:68
  752.9 530.7 %while.48 = (s32[]{:T(128)}, f32[2048,8,64]{0,2,1:T(8,128)}, f32[2048,8,64]{0,2,1:T(8,128)}, f32[4,512,8,64]{1,0,3,2:T(4,128)}, bf16[4,512,8,64]{1,3,2,0:T(8,128...) while((s32[]{:T(128)}, f32[2048,8,64]{0,2,1:T(8,128)}, ...), condition=%wide.region_12.13_spmd.clone, body=%wide.region_10.12_spmd.clone.sunk | while | flops 5451807232 | bytes 355557600 | solution.py:162
  756.7 18.0 %fusion.130 = f32[8,512,2048]{2,1,0:T(8,128)} fusion(bf16[2048,8,64]{0,2,1:T(8,128)(2,1)} %get-tuple-element.605, bf16[4,512,8,64]{1,3,2,0:T(8,128)(2,1)} %get-tuple-element.604, s32[]{:T(128)S(6)} %copy.120), kind=kOutput, calls=%fused_computation.31.clone.1 | convolution fusion | flops 1073741824 | bytes 36175876 | tf_op jit(solution)/shard_map/while/body/eval_jaxpr/while/body/eval_jaxpr/qhd,khd->hqk/dot_general | solution.py:133
  774.7 24.9 %multiply_reduce_fusion.5 = (f32[8,512]{1,0:T(8,128)S(1)}, f32[8,512,2048]{2,1,0:T(8,128)}) fusion(f32[8,512,2048]{2,1,0:T(8,128)} %fusion.130, f32[8,512]{1,0:T(8,128)S(1)} %dynamic-slice_bitcast_fusion.2, bf16[2048,8,64]{0,2,1:T(8,128)(2,1)S(1)} %get-tuple-element.602, bf16[4,512,8,64]{1,3,2,0:T(8,128)(2,1)} %get-tuple-element.599, ...), kind=kOutput, calls=%fused_computation.20.clone.1 | convolution fusion | flops 1115680768 | bytes 70811648 | tf_op jit(solution)/shard_map/while/body/eval_jaxpr/while/body/eval_jaxpr/qhd,khd->hqk/dot_general | solution.py:77
  799.6 28.3 %multiply_convert_fusion.10 = bf16[8,512,2048]{2,1,0:T(8,128)(2,1)} fusion(f32[8,512,2048]{2,1,0:T(8,128)} %get-tuple-element.540, f32[8,512,2048]{2,1,0:T(8,128)} %fusion.130, f32[8,512]{1,0:T(8,128)S(1)} %get-tuple-element.541), kind=kLoop, calls=%fused_computation.19.clone.1 | loop fusion | flops 25165824 | bytes 83902464 | tf_op jit(solution)/shard_map/while/body/eval_jaxpr/while/body/eval_jaxpr/convert_element_type | solution.py:137
  863.5 21.2 %dynamic_update_slice.31 = f32[4,512,8,64]{1,0,3,2:T(4,128)} dynamic-update-slice(f32[4,512,8,64]{1,0,3,2:T(4,128)} %get-tuple-element.585, f32[1,512,8,64]{1,0,3,2:T(1,128)} %copy.102, s32[]{:T(128)S(6)} %copy.120, s32[]{:T(128)} %constant.92.clone.1..sunk, s32[]{:T(128)} %constant.92.clone.1..sunk, s32[]{:T(128)} %constant.92.clone.1..sunk) | dynamic-update-slice | bytes 2097156 | tf_op jit(solution)/shard_map/while/body/eval_jaxpr/while/body/jit(dynamic_update_index_in_dim)/dynamic_update_slice | solution.py:110
  888.1 17.9 %fusion.130 = f32[8,512,2048]{2,1,0:T(8,128)} fusion(bf16[2048,8,64]{0,2,1:T(8,128)(2,1)} %get-tuple-element.605, bf16[4,512,8,64]{1,3,2,0:T(8,128)(2,1)} %get-tuple-element.604, s32[]{:T(128)S(6)} %copy.120), kind=kOutput, calls=%fused_computation.31.clone.1 | convolution fusion | flops 1073741824 | bytes 36175876 | tf_op jit(solution)/shard_map/while/body/eval_jaxpr/while/body/eval_jaxpr/qhd,khd->hqk/dot_general | solution.py:133
  906.0 24.9 %multiply_reduce_fusion.5 = (f32[8,512]{1,0:T(8,128)S(1)}, f32[8,512,2048]{2,1,0:T(8,128)}) fusion(f32[8,512,2048]{2,1,0:T(8,128)} %fusion.130, f32[8,512]{1,0:T(8,128)S(1)} %dynamic-slice_bitcast_fusion.2, bf16[2048,8,64]{0,2,1:T(8,128)(2,1)S(1)} %get-tuple-element.602, bf16[4,512,8,64]{1,3,2,0:T(8,128)(2,1)} %get-tuple-element.599, ...), kind=kOutput, calls=%fused_computation.20.clone.1 | convolution fusion | flops 1115680768 | bytes 70811648 | tf_op jit(solution)/shard_map/while/body/eval_jaxpr/while/body/eval_jaxpr/qhd,khd->hqk/dot_general | solution.py:77
  930.9 28.0 %multiply_convert_fusion.10 = bf16[8,512,2048]{2,1,0:T(8,128)(2,1)} fusion(f32[8,512,2048]{2,1,0:T(8,128)} %get-tuple-element.540, f32[8,512,2048]{2,1,0:T(8,128)} %fusion.130, f32[8,512]{1,0:T(8,128)S(1)} %get-tuple-element.541), kind=kLoop, calls=%fused_computation.19.clone.1 | loop fusion | flops 25165824 | bytes 83902464 | tf_op jit(solution)/shard_map/while/body/eval_jaxpr/while/body/eval_jaxpr/convert_element_type | solution.py:137
  958.8 18.1 %bitcast_add_fusion.5 = f32[2048,8,64]{0,2,1:T(8,128)} fusion(f32[2048,8,64]{0,2,1:T(8,128)} %get-tuple-element.584, f32[8,512,2048]{2,1,0:T(8,128)} %get-tuple-element.540, pred[]{:T(512)S(6)} %compare.18, bf16[4,512,8,64]{1,3,2,0:T(8,128)(2,1)} %get-tuple-element.604, s32[]{:T(128)S(6)} %copy.120), kind=kOutput, calls=%fused_computation.24.clone.1 | convolution fusion | flops 1084227584 | bytes 42467332 | tf_op jit(solution)/shard_map/while/body/eval_jaxpr/while/body/eval_jaxpr/hqk,qhd->khd/dot_general | solution.py:151
  998.9 21.1 %dynamic_update_slice.31 = f32[4,512,8,64]{1,0,3,2:T(4,128)} dynamic-update-slice(f32[4,512,8,64]{1,0,3,2:T(4,128)} %get-tuple-element.585, f32[1,512,8,64]{1,0,3,2:T(1,128)} %copy.102, s32[]{:T(128)S(6)} %copy.120, s32[]{:T(128)} %constant.92.clone.1..sunk, s32[]{:T(128)} %constant.92.clone.1..sunk, s32[]{:T(128)} %constant.92.clone.1..sunk) | dynamic-update-slice | bytes 2097156 | tf_op jit(solution)/shard_map/while/body/eval_jaxpr/while/body/jit(dynamic_update_index_in_dim)/dynamic_update_slice | solution.py:110
  1023.4 17.7 %fusion.130 = f32[8,512,2048]{2,1,0:T(8,128)} fusion(bf16[2048,8,64]{0,2,1:T(8,128)(2,1)} %get-tuple-element.605, bf16[4,512,8,64]{1,3,2,0:T(8,128)(2,1)} %get-tuple-element.604, s32[]{:T(128)S(6)} %copy.120), kind=kOutput, calls=%fused_computation.31.clone.1 | convolution fusion | flops 1073741824 | bytes 36175876 | tf_op jit(solution)/shard_map/while/body/eval_jaxpr/while/body/eval_jaxpr/qhd,khd->hqk/dot_general | solution.py:133
  1041.1 24.7 %multiply_reduce_fusion.5 = (f32[8,512]{1,0:T(8,128)S(1)}, f32[8,512,2048]{2,1,0:T(8,128)}) fusion(f32[8,512,2048]{2,1,0:T(8,128)} %fusion.130, f32[8,512]{1,0:T(8,128)S(1)} %dynamic-slice_bitcast_fusion.2, bf16[2048,8,64]{0,2,1:T(8,128)(2,1)S(1)} %get-tuple-element.602, bf16[4,512,8,64]{1,3,2,0:T(8,128)(2,1)} %get-tuple-element.599, ...), kind=kOutput, calls=%fused_computation.20.clone.1 | convolution fusion | flops 1115680768 | bytes 70811648 | tf_op jit(solution)/shard_map/while/body/eval_jaxpr/while/body/eval_jaxpr/qhd,khd->hqk/dot_general | solution.py:77
  1065.8 27.5 %multiply_convert_fusion.10 = bf16[8,512,2048]{2,1,0:T(8,128)(2,1)} fusion(f32[8,512,2048]{2,1,0:T(8,128)} %get-tuple-element.540, f32[8,512,2048]{2,1,0:T(8,128)} %fusion.130, f32[8,512]{1,0:T(8,128)S(1)} %get-tuple-element.541), kind=kLoop, calls=%fused_computation.19.clone.1 | loop fusion | flops 25165824 | bytes 83902464 | tf_op jit(solution)/shard_map/while/body/eval_jaxpr/while/body/eval_jaxpr/convert_element_type | solution.py:137
  1130.8 21.1 %dynamic_update_slice.31 = f32[4,512,8,64]{1,0,3,2:T(4,128)} dynamic-update-slice(f32[4,512,8,64]{1,0,3,2:T(4,128)} %get-tuple-element.585, f32[1,512,8,64]{1,0,3,2:T(1,128)} %copy.102, s32[]{:T(128)S(6)} %copy.120, s32[]{:T(128)} %constant.92.clone.1..sunk, s32[]{:T(128)} %constant.92.clone.1..sunk, s32[]{:T(128)} %constant.92.clone.1..sunk) | dynamic-update-slice | bytes 2097156 | tf_op jit(solution)/shard_map/while/body/eval_jaxpr/while/body/jit(dynamic_update_index_in_dim)/dynamic_update_slice | solution.py:110
  1155.3 17.4 %fusion.130 = f32[8,512,2048]{2,1,0:T(8,128)} fusion(bf16[2048,8,64]{0,2,1:T(8,128)(2,1)} %get-tuple-element.605, bf16[4,512,8,64]{1,3,2,0:T(8,128)(2,1)} %get-tuple-element.604, s32[]{:T(128)S(6)} %copy.120), kind=kOutput, calls=%fused_computation.31.clone.1 | convolution fusion | flops 1073741824 | bytes 36175876 | tf_op jit(solution)/shard_map/while/body/eval_jaxpr/while/body/eval_jaxpr/qhd,khd->hqk/dot_general | solution.py:133
  1172.7 24.7 %multiply_reduce_fusion.5 = (f32[8,512]{1,0:T(8,128)S(1)}, f32[8,512,2048]{2,1,0:T(8,128)}) fusion(f32[8,512,2048]{2,1,0:T(8,128)} %fusion.130, f32[8,512]{1,0:T(8,128)S(1)} %dynamic-slice_bitcast_fusion.2, bf16[2048,8,64]{0,2,1:T(8,128)(2,1)S(1)} %get-tuple-element.602, bf16[4,512,8,64]{1,3,2,0:T(8,128)(2,1)} %get-tuple-element.599, ...), kind=kOutput, calls=%fused_computation.20.clone.1 | convolution fusion | flops 1115680768 | bytes 70811648 | tf_op jit(solution)/shard_map/while/body/eval_jaxpr/while/body/eval_jaxpr/qhd,khd->hqk/dot_general | solution.py:77
  1197.3 27.5 %multiply_convert_fusion.10 = bf16[8,512,2048]{2,1,0:T(8,128)(2,1)} fusion(f32[8,512,2048]{2,1,0:T(8,128)} %get-tuple-element.540, f32[8,512,2048]{2,1,0:T(8,128)} %fusion.130, f32[8,512]{1,0:T(8,128)S(1)} %get-tuple-element.541), kind=kLoop, calls=%fused_computation.19.clone.1 | loop fusion | flops 25165824 | bytes 83902464 | tf_op jit(solution)/shard_map/while/body/eval_jaxpr/while/body/eval_jaxpr/convert_element_type | solution.py:137
  1262.4 21.1 %dynamic_update_slice.31 = f32[4,512,8,64]{1,0,3,2:T(4,128)} dynamic-update-slice(f32[4,512,8,64]{1,0,3,2:T(4,128)} %get-tuple-element.585, f32[1,512,8,64]{1,0,3,2:T(1,128)} %copy.102, s32[]{:T(128)S(6)} %copy.120, s32[]{:T(128)} %constant.92.clone.1..sunk, s32[]{:T(128)} %constant.92.clone.1..sunk, s32[]{:T(128)} %constant.92.clone.1..sunk) | dynamic-update-slice | bytes 2097156 | tf_op jit(solution)/shard_map/while/body/eval_jaxpr/while/body/jit(dynamic_update_index_in_dim)/dynamic_update_slice | solution.py:110
  1371.4 41.1 %reduce-scatter.14.cloned.1.call-done = bf16[1024,1024]{1,0:T(8,128)(2,1)} async-done(((bf16[2048,1024]{1,0:T(8,128)(2,1)}), bf16[1024,1024]{1,0:T(8,128)(2,1)}) %reduce-scatter.14.cloned.1.call-update) | async-done | bytes 2097168 | tf_op jit(solution)/shard_map/reduce_scatter | solution.py:295
  1416.4 39.9 %psum.7 = f32[2,1024]{1,0:T(2,128)S(1)} all-reduce(f32[2,1024]{1,0:T(2,128)S(1)} %pad_maximum_fusion.4), channel_id=1, replica_groups=mesh['dp'=16,'mp'=2] {'dp','mp'}, use_global_device_ids=true, to_apply=%region_21.22 | all-reduce | flops 2048 | bytes 16384 | tf_op jit(solution)/shard_map/psum | solution.py:310
  1457.0 58.5 %reduce-scatter.10.cloned.1.call-done = f32[1024,1024]{1,0:T(8,128)} async-done(((f32[2048,1024]{1,0:T(8,128)}), f32[1024,1024]{1,0:T(8,128)}) %reduce-scatter.10.cloned.1.call-update) | async-done | bytes 4194320 | tf_op jit(solution)/shard_map/reduce_scatter | solution.py:257
  1525.9 78.8 %reduce-scatter.16.cloned.1.call-done = f32[64,3,512]{2,0,1:T(8,128)} async-done(((f32[1024,3,512]{2,0,1:T(8,128)}), f32[64,3,512]{2,0,1:T(8,128)}) %reduce-scatter.16.cloned.1.call-update) | async-done | bytes 393232 | tf_op jit(solution)/shard_map/reduce_scatter | solution.py:301
  (285 shorter events, 584.1 us)
Async XLA Ops:
  7.2 61.9 %all-gather.5.cloned.1.call-start = ((), (), s32[]{:S(2)}) async-start(), calls=%async_computation.7 | async-start | bytes 6291456 | tf_op jit(solution)/shard_map/all_gather | solution.py:229
  7.9 399.8 %reduce-scatter.8.cloned.1.call-start = ((), (), s32[]{:S(2)}) async-start(), calls=%async_computation.8 | async-start | bytes 12582912 | tf_op jit(solution)/shard_map/reduce_scatter | solution.py:243
  12.0 60.3 %copy-start.19 = (bf16[1024,3,512]{0,2,1:T(8,128)(2,1)}, bf16[1024,3,512]{0,2,1:T(8,128)(2,1)S(1)}, u32[]{:S(2)}) copy-start(bf16[1024,3,512]{0,2,1:T(8,128)(2,1)S(1)} %copy.67) | copy-start | bytes 9437188
  17.4 65.1 %copy-start.45 = (f32[1,1024]{1,0:T(1,128)}, f32[1,1024]{1,0:T(1,128)S(1)}, u32[]{:S(2)}) copy-start(f32[1,1024]{1,0:T(1,128)S(1)} %get-tuple-element.413) | copy-start | bytes 12292
  19.2 72.5 %copy-start.23 = (f32[2048,32]{0,1:T(8,128)}, f32[2048,32]{0,1:T(8,128)S(1)}, u32[]{:S(2)}) copy-start(f32[2048,32]{0,1:T(8,128)S(1)} %get-tuple-element.414) | copy-start | bytes 786436
  308.3 99.4 %copy-start.14 = (bf16[1024,1024]{1,0:T(8,128)(2,1)S(1)}, bf16[1024,1024]{1,0:T(8,128)(2,1)}, u32[]{:S(2)}) copy-start(bf16[1024,1024]{1,0:T(8,128)(2,1)} %param.23) | copy-start | bytes 6291460
  308.3 104.2 %copy-start.37 = (f32[1,1024]{1,0:T(1,128)S(1)}, f32[1,1024]{1,0:T(1,128)}, u32[]{:S(2)}) copy-start(f32[1,1024]{1,0:T(1,128)} %get-tuple-element.412) | copy-start | bytes 12292
  308.3 162.9 %all-gather.7.cloned.1.call-start = ((), (), s32[]{:S(2)}) async-start(), calls=%async_computation.9 | async-start | bytes 6291456 | tf_op jit(solution)/shard_map/all_gather | solution.py:250
  410.5 264.5 %copy-start.35 = (f32[1024]{0:T(1024)}, f32[1024]{0:T(1024)S(1)}, u32[]{:S(2)}) copy-start(f32[1024]{0:T(1024)S(1)} %add_rsqrt_fusion.1) | copy-start | bytes 12292
  414.3 115.7 %all-gather.9.cloned.1.call-start = ((), (), s32[]{:S(2)}) async-start(), calls=%async_computation.11 | async-start | bytes 6291456 | tf_op jit(solution)/shard_map/all_gather | solution.py:265
  415.0 260.0 %copy-start.39 = (f32[1024]{0:T(1024)}, f32[1024]{0:T(1024)S(1)}, u32[]{:S(2)}) copy-start(f32[1024]{0:T(1024)S(1)} %fusion.64) | copy-start | bytes 12292
  416.8 252.9 %reduce-scatter.12.cloned.1.call-start = ((), (), s32[]{:S(2)}) async-start(), calls=%async_computation.12 | async-start | bytes 12582912 | tf_op jit(solution)/shard_map/reduce_scatter | solution.py:272
  570.3 164.8 %all-gather.11.cloned.1.call-start = ((), (), s32[]{:S(2)}) async-start(), calls=%async_computation.13 | async-start | bytes 6291456 | tf_op jit(solution)/shard_map/all_gather | solution.py:279
  678.2 673.8 %all-reduce.3.cloned.1.call-start = ((), (), s32[]{:S(2)}) async-start(), calls=%async_computation.18 | async-start | bytes 23068672
  712.5 644.2 %reduce-scatter.20.cloned.1.call-start = ((), (), s32[]{:S(2)}) async-start(), calls=%async_computation.17 | async-start | bytes 6127616 | tf_op jit(solution)/shard_map/reduce_scatter | solution.py:308
  724.3 645.2 %reduce-scatter.18.cloned.1.call-start = ((), (), s32[]{:S(2)}) async-start(), calls=%async_computation.16 | async-start | bytes 2228224 | tf_op jit(solution)/shard_map/reduce_scatter | solution.py:304
  976.9 11.7 copy-start
  1295.9 116.6 %reduce-scatter.14.cloned.1.call-start = ((), (), s32[]{:S(2)}) async-start(), calls=%async_computation.14 | async-start | bytes 6291456 | tf_op jit(solution)/shard_map/reduce_scatter | solution.py:295
  1315.5 200.0 %reduce-scatter.10.cloned.1.call-start = ((), (), s32[]{:S(2)}) async-start(), calls=%async_computation.10 | async-start | bytes 12582912 | tf_op jit(solution)/shard_map/reduce_scatter | solution.py:257
  1328.0 276.7 %reduce-scatter.16.cloned.1.call-start = ((), (), s32[]{:S(2)}) async-start(), calls=%async_computation.15 | async-start | bytes 6684672 | tf_op jit(solution)/shard_map/reduce_scatter | solution.py:301
  1369.4 47.0 %copy-start.49 = (f32[1024]{0:T(1024)S(1)}, f32[1024]{0:T(1024)}, u32[]{:S(2)}) copy-start(f32[1024]{0:T(1024)} %get-tuple-element.327) | copy-start | bytes 12292
  1369.4 87.0 %copy-start.48 = (f32[2,1024]{1,0:T(2,128)S(1)}, f32[2,1024]{1,0:T(2,128)}, u32[]{:S(2)}) copy-start(f32[2,1024]{1,0:T(2,128)} %param.31) | copy-start | bytes 24580
  1369.4 87.0 %copy-start.50 = (f32[2,1024]{1,0:T(2,128)S(1)}, f32[2,1024]{1,0:T(2,128)}, u32[]{:S(2)}) copy-start(f32[2,1024]{1,0:T(2,128)} %param.41) | copy-start | bytes 24580
  1369.4 87.0 %copy-start.51 = (f32[2,1024]{1,0:T(2,128)S(1)}, f32[2,1024]{1,0:T(2,128)}, u32[]{:S(2)}) copy-start(f32[2,1024]{1,0:T(2,128)} %param.36) | copy-start | bytes 24580
  1369.4 146.1 %copy-start.11 = (bf16[1024,1024]{1,0:T(8,128)(2,1)S(1)}, bf16[1024,1024]{1,0:T(8,128)(2,1)}, u32[]{:S(2)}) copy-start(bf16[1024,1024]{1,0:T(8,128)(2,1)} %param.26) | copy-start | bytes 6291460
  1369.4 146.1 %copy-start.36 = (f32[1024]{0:T(1024)S(1)}, f32[1024]{0:T(1024)}, u32[]{:S(2)}) copy-start(f32[1024]{0:T(1024)} %copy-done.35) | copy-start | bytes 12292
  1369.4 146.1 %copy-start.38 = (f32[1,1024]{1,0:T(1,128)S(1)}, f32[1,1024]{1,0:T(1,128)}, u32[]{:S(2)}) copy-start(f32[1,1024]{1,0:T(1,128)} %get-tuple-element.412) | copy-start | bytes 12292
  1369.4 146.1 %copy-start.40 = (f32[1024]{0:T(1024)S(1)}, f32[1024]{0:T(1024)}, u32[]{:S(2)}) copy-start(f32[1024]{0:T(1024)} %copy-done.39) | copy-start | bytes 12292
  1369.4 146.1 %dynamic-slice-start = ((f32[2048]{0:T(1024)}, s32[]{:T(128)}), f32[1024]{0:T(1024)S(1)}, s32[]{:S(2)}) async-start(f32[2048]{0:T(1024)} %copy-done.41, s32[]{:T(128)} %select_n.53), calls=%async_computation.19 | async-start | bytes 8704 | tf_op jit(solution)/shard_map/dynamic-slice.1
  1369.5 146.1 %copy-start.44 = (f32[1024]{0:T(1024)S(1)}, f32[1024]{0:T(1024)}, u32[]{:S(2)}) copy-start(f32[1024]{0:T(1024)} %copy-done.43) | copy-start | bytes 12292
  1457.0 147.8 %copy-start.29 = (f32[64,3,512]{2,0,1:T(8,128)S(1)}, f32[64,3,512]{2,0,1:T(8,128)}, u32[]{:S(2)}) copy-start(f32[64,3,512]{2,0,1:T(8,128)} %param.37) | copy-start | bytes 1179652
  1457.0 147.8 %copy-start.30 = (f32[64,3,512]{2,0,1:T(8,128)S(1)}, f32[64,3,512]{2,0,1:T(8,128)}, u32[]{:S(2)}) copy-start(f32[64,3,512]{2,0,1:T(8,128)} %param.32) | copy-start | bytes 1179652
  (42 other events, 207.5 us)
Sparse Core Ops, SparseCore 0:
  9.6 59.4 all-gather.4
  308.4 99.2 reduce-scatter.7
  414.4 56.7 all-gather.6
  473.2 56.7 all-gather.8
  570.4 99.2 reduce-scatter.11
  678.3 56.7 all-gather.10
  738.9 217.7 all-reduce.2
  960.5 81.4 reduce-scatter.19
  1296.0 60.9 reduce-scatter.17
  1359.2 53.2 reduce-scatter.13
  1414.8 100.6 reduce-scatter.9
  1519.8 84.9 reduce-scatter.15
where the time goes:
time: 1630 us; the launch traced here: 1610 us
  matrix products  582 us (36%)
  waiting for transfers between devices  521 us (32%)
  other arithmetic  269 us (17%)
  local copies, waits for them, and re-layouts  184 us (11%)
  blocking collectives  39.9 us (2%)
  between operations  16.3 us (1%)
    dot_general x8, matrix products, block_scores(): jnp.einsum('qhd,khd->hqk', query_block, keys, preferred_element_type=jnp....  158 us
    convert_element_type x4, other arithmetic, per_block(): score_grad = (probs * (prob_grad - center)).astype(jnp.bfloat16)  111 us
    reduce_scatter x1, waiting for transfers between devices, shards(): lax.psum_scatter(dot_last(grad_gateup_bf, gateup_bf), 'mp', scatter_dimen...  99.3 us
    reduce_scatter x1, waiting for transfers between devices, shards(): lax.psum_scatter(jnp.dot(mixed_bf, out_bf, preferred_element_type=jnp.flo...  98.9 us
    dynamic_update_slice x8, local copies, waits for them, and re-layouts, per_slot(): lax.map(per_block, (slot_queries.reshape(blocks, block_len, heads_here, h...  92.9 us
    reduce_scatter x1, waiting for transfers between devices, shards(): lax.psum_scatter(grad_qkv.reshape(model, 3, head_cols), 'dp', scatter_dim...  78.8 us
    dot_general x4, matrix products, per_block(): jnp.einsum('qhd,khd->hqk', grad_block, slot_values, preferred_element_typ...  71 us
    dot_general x4, matrix products, per_block(): jnp.einsum('hqk,qhd->khd', probs.astype(jnp.bfloat16), grad_block, prefer...  67.8 us
  transfers between devices with their start and end apart: 12, of which 9 were waited for; matrix products, arithmetic and copies ran while one was open for 45% of the time, Pallas kernels for 0%

commit v1 on v0

--- a/solution.py
+++ b/solution.py
@@ -1,8 +1,11 @@
+import functools
 import math
 
 import jax
 import jax.numpy as jnp
 from jax import lax
+from jax.experimental import pallas as pl
+from jax.experimental.pallas import tpu as pltpu
 from jax.sharding import PartitionSpec as P
 
 HEAD_DIM = 64
@@ -183,7 +186,7 @@
     return (grad, moment_new, average_new, weight_new)
 
 
-def shards(
+def shards_any(
     tokens,
     first_values,
     lengths,
@@ -347,6 +350,952 @@
     )
 
 
+F32 = jnp.float32
+BF16 = jnp.bfloat16
+LANES = 128
+BLK = 256
+PARTS = 3
+SWAP = ((0, 1), (1, 0))
+VMEM_MIB = 60
+
+
+def nt(left, right):
+    return lax.dot_general(left, right, (((1,), (1,)), ((), ())), preferred_element_type=F32)
+
+
+def nn(left, right):
+    return lax.dot_general(left, right, (((1,), (0,)), ((), ())), preferred_element_type=F32)
+
+
+def tn(left, right):
+    return lax.dot_general(left, right, (((0,), (0,)), ((), ())), preferred_element_type=F32)
+
+
+def lane_of(rows):
+    return lax.broadcasted_iota(jnp.int32, (rows, LANES), 1)
+
+
+def params(mib):
+    return pltpu.CompilerParams(vmem_limit_bytes=mib * 2**20)
+
+
+def cost(flops, moved, exps=0):
+    return pl.CostEstimate(flops=int(flops), bytes_accessed=int(moved), transcendentals=int(exps))
+
+
+def partner_lanes(pair):
+    lane = lane_of(pair.shape[0])
+    return jnp.where((lane % HEAD_DIM) < HEAD_DIM // 2, pltpu.roll(pair, LANES - 32, 1), pltpu.roll(pair, 32, 1))
+
+
+def pair_tables(length):
+    cosine, sine = rope_tables(length, HEAD_DIM)
+    cosine, sine = cosine[:, 0, :], sine[:, 0, :]
+    wide_cos = jnp.concatenate([cosine] * 4, axis=1)
+    wide_sin = jnp.concatenate([-sine, sine, -sine, sine], axis=1)
+    return wide_cos, wide_sin
+
+
+def qkv_kernel(base_ref, x_ref, first_ref, gain_ref, w_ref, cos_ref, sin_ref, *refs):
+    n_ref, q_ref, k_ref, v_ref = refs[-4:]
+    x = x_ref[...].astype(F32)
+    inverse = lax.rsqrt(jnp.mean(x * x, axis=-1, keepdims=True) + EPS)
+    norm = ((x * inverse) * gain_ref[...]).astype(BF16)
+    n_ref[...] = norm
+    cosine, sine = cos_ref[...], sin_ref[...]
+    for part, out in ((0, q_ref), (1, k_ref)):
+        flat = nn(norm, w_ref[part])
+        for c in range(flat.shape[1] // LANES):
+            pair = flat[:, c * LANES : (c + 1) * LANES]
+            turned = (pair * cosine + partner_lanes(pair) * sine).astype(BF16)
+            if part == 0:
+                turned = turned * jnp.asarray(0.125, BF16)
+            out[:, c * LANES : (c + 1) * LANES] = turned
+    v_ref[...] = (HALF * nn(norm, w_ref[2]) + HALF * first_ref[...].astype(F32)).astype(BF16)
+
+
+def project_qkv(base, x, first, gain, w, cosine, sine, before):
+    rows, model = x.shape
+    slot_len, cols = first.shape
+    here = lambda i, b: (i, 0)
+    there = lambda i, b: (b[0] + i, 0)
+    outs = (
+        jax.ShapeDtypeStruct((slot_len, model), BF16),
+        *(jax.ShapeDtypeStruct((slot_len, cols), BF16) for _ in range(3)),
+    )
+    before = () if before is None else tuple(before)
+    return pl.pallas_call(
+        qkv_kernel,
+        out_shape=outs,
+        grid_spec=pltpu.PrefetchScalarGridSpec(
+            num_scalar_prefetch=1,
+            grid=(rows // BLK,),
+            in_specs=[
+                pl.BlockSpec((BLK, model), here),
+                pl.BlockSpec((BLK, cols), there),
+                pl.BlockSpec((1, model), lambda i, b: (0, 0)),
+                pl.BlockSpec((PARTS, model, cols), lambda i, b: (0, 0, 0)),
+                pl.BlockSpec((BLK, LANES), there),
+                pl.BlockSpec((BLK, LANES), there),
+                *(pl.BlockSpec(memory_space=pl.ANY) for _ in before),
+            ],
+            out_specs=[pl.BlockSpec((BLK, o.shape[1]), there) for o in outs],
+        ),
+        input_output_aliases={7 + n: n for n in range(len(before))},
+        compiler_params=params(VMEM_MIB),
+        cost_estimate=cost(2 * rows * model * cols * 3, 10e6),
+        name="project_qkv",
+    )(base, x, first, gain, w, cosine, sine, *before)
+
+
+def attend_fwd_kernel(len_ref, q_ref, k_ref, v_ref, *refs):
+    o_ref, lse_ref, ka_ref, va_ref, mask_ref = refs[-5:]
+    block = pl.program_id(0)
+    slot_len = k_ref.shape[0]
+
+    @pl.when(block == 0)
+    def _():
+        row = lax.broadcasted_iota(jnp.int32, (slot_len, LANES), 0)
+        lane = lane_of(slot_len)
+        bias = jnp.where(row < len_ref[0], 0.0, NEG_BIG).astype(BF16)
+        for head in (0, 1):
+            mine = (lane // HEAD_DIM) == head
+            spot = HEAD_DIM * (1 - head)
+            ka_ref[head] = jnp.where(mine, k_ref[...], jnp.where(lane == spot, bias, jnp.zeros_like(bias)))
+            va_ref[head] = jnp.where(mine, v_ref[...], jnp.ones_like(bias))
+        query = lax.broadcasted_iota(jnp.int32, (BLK, BLK), 0)
+        key = lax.broadcasted_iota(jnp.int32, (BLK, BLK), 1)
+        mask_ref[...] = jnp.where(key <= query, 0.0, NEG_BIG)
+
+    lane = lane_of(BLK)
+    low = lane < HEAD_DIM
+    for count in range(slot_len // BLK):
+
+        @pl.when(block == count)
+        def _():
+            q = q_ref[...]
+            outs, peaks = [], []
+            for head in (0, 1):
+                spot = HEAD_DIM * (1 - head)
+                one = jnp.where(lane == spot, 1.0, 0.0).astype(BF16)
+                scored = jnp.where((lane // HEAD_DIM) == head, q, one)
+                scores = []
+                for j in range(count + 1):
+                    s = nt(scored, ka_ref[head, pl.ds(j * BLK, BLK), :])
+                    scores.append(s + mask_ref[...] if j == count else s)
+                top = scores[0]
+                for s in scores[1:]:
+                    top = jnp.maximum(top, s)
+                peak = jnp.max(top, axis=1, keepdims=True)
+                acc = None
+                for j, s in enumerate(scores):
+                    p = jnp.exp(s - peak).astype(BF16)
+                    term = nn(p, va_ref[head, pl.ds(j * BLK, BLK), :])
+                    acc = term if acc is None else acc + term
+                outs.append(acc)
+                peaks.append(peak)
+            total = pltpu.roll(jnp.where(low, outs[1], outs[0]), HEAD_DIM, 1)
+            o_ref[...] = (jnp.where(low, outs[0], outs[1]) / total).astype(BF16)
+            lse_ref[...] = jnp.where(low, peaks[0], peaks[1]) + jnp.log(total)
+
+
+def attend_pair(pair, length, q, k, v, before):
+    slot_len, cols = q.shape
+    blocks = slot_len // BLK
+    row = pl.BlockSpec((BLK, LANES), lambda i, n: (i, pair))
+    full = pl.BlockSpec((slot_len, LANES), lambda i, n: (0, pair))
+    before = () if before is None else tuple(before)
+    return pl.pallas_call(
+        attend_fwd_kernel,
+        out_shape=(
+            jax.ShapeDtypeStruct((slot_len, cols), BF16),
+            jax.ShapeDtypeStruct((slot_len, cols), F32),
+        ),
+        grid_spec=pltpu.PrefetchScalarGridSpec(
+            num_scalar_prefetch=1,
+            grid=(blocks,),
+            in_specs=[row, full, full] + [pl.BlockSpec(memory_space=pl.ANY) for _ in before],
+            out_specs=[row, row],
+            scratch_shapes=[
+                pltpu.VMEM((2, slot_len, LANES), BF16),
+                pltpu.VMEM((2, slot_len, LANES), BF16),
+                pltpu.VMEM((BLK, BLK), F32),
+            ],
+        ),
+        input_output_aliases={4 + n: n for n in range(len(before))},
+        compiler_params=params(VMEM_MIB),
+        cost_estimate=cost(2 * 2 * slot_len * slot_len * 256, 3e6),
+        name="attend_pair",
+    )(length, q, k, v, *before)
+
+
+def split3(x):
+    high = x.astype(BF16)
+    rest = x - high.astype(F32)
+    mid = rest.astype(BF16)
+    return high, mid, (rest - mid.astype(F32)).astype(BF16)
+
+
+def attend_back_kernel(len_ref, q_ref, k_ref, v_ref, do_ref, o_ref, lse_ref, cos_ref, sin_ref, *refs):
+    fv_ref, grad_ref, send_ref, qa, ka, va, da, qz, kz, dz, mask_ref, dq_acc = refs[-12:]
+    slot_len = k_ref.shape[0]
+    blocks = slot_len // BLK
+    lane = lane_of(slot_len)
+    low = lane < HEAD_DIM
+    row = lax.broadcasted_iota(jnp.int32, (slot_len, LANES), 0)
+    bias = jnp.where(row < len_ref[0], 0.0, NEG_BIG).astype(BF16)
+    zero = jnp.zeros_like(bias)
+    minus = jnp.full_like(bias, -1.0)
+    prod = do_ref[...].astype(F32) * o_ref[...].astype(F32)
+    center_low = jnp.sum(jnp.where(low, prod, 0.0), axis=1, keepdims=True)
+    center_high = jnp.sum(jnp.where(low, 0.0, prod), axis=1, keepdims=True)
+    centers = split3(jnp.where(low, center_high, center_low))
+    totals = split3(pltpu.roll(lse_ref[...], HEAD_DIM, 1))
+
+    def place(head, items):
+        out = zero
+        for n, item in enumerate(items):
+            out = jnp.where(lane == HEAD_DIM * (1 - head) + n, item, out)
+        return out
+
+    for head in (0, 1):
+        mine = (lane // HEAD_DIM) == head
+        qa[head] = jnp.where(mine, q_ref[...], place(head, [-minus, *totals]))
+        ka[head] = jnp.where(mine, k_ref[...], place(head, [bias, minus, minus, minus]))
+        da[head] = jnp.where(mine, do_ref[...], place(head, centers))
+        va[head] = jnp.where(mine, v_ref[...], place(head, [minus, minus, minus]))
+        qz[head] = jnp.where(mine, q_ref[...], zero)
+        kz[head] = jnp.where(mine, k_ref[...], zero)
+        dz[head] = jnp.where(mine, do_ref[...], zero)
+    key = lax.broadcasted_iota(jnp.int32, (BLK, BLK), 0)
+    query = lax.broadcasted_iota(jnp.int32, (BLK, BLK), 1)
+    mask_ref[...] = jnp.where(key <= query, 0.0, NEG_BIG)
+    dq_acc[...] = jnp.zeros_like(dq_acc)
+
+    def unturn(grad, rows):
+        return grad * cos_ref[rows, :] - partner_lanes(grad) * sin_ref[rows, :]
+
+    for j in range(blocks):
+        keys = pl.ds(j * BLK, BLK)
+        dk = dv = None
+        for i in range(j, blocks):
+            queries = pl.ds(i * BLK, BLK)
+            dq = None
+            for head in (0, 1):
+                s = nt(ka[head, keys, :], qa[head, queries, :])
+                if i == j:
+                    s = s + mask_ref[...]
+                p = jnp.exp(s)
+                ds = (p * nt(va[head, keys, :], da[head, queries, :])).astype(BF16)
+                term = nn(p.astype(BF16), dz[head, queries, :])
+                dv = term if dv is None else dv + term
+                term = nn(ds, qz[head, queries, :])
+                dk = term if dk is None else dk + term
+                term = tn(ds, kz[head, keys, :])
+                dq = term if dq is None else dq + term
+            dq_acc[queries, :] += dq
+        half_dv = HALF * dv
+        fv_ref[keys, :] = half_dv
+        grad_ref[keys, 2 * LANES : 3 * LANES] = half_dv.astype(BF16)
+        grad_ref[keys, LANES : 2 * LANES] = unturn(dk, keys).astype(BF16)
+    for i in range(blocks):
+        queries = pl.ds(i * BLK, BLK)
+        grad_ref[queries, 0:LANES] = unturn(dq_acc[queries, :] * 0.125, queries).astype(BF16)
+    send_ref[...] = grad_ref[pl.ds(pl.multiple_of(len_ref[1] * BLK, BLK), send_ref.shape[0]), :]
+
+
+def attend_back_pair(pair, length, q, k, v, do, o, lse, cosine, sine, before):
+    slot_len, cols = q.shape
+    full = pl.BlockSpec((slot_len, LANES), lambda i, n: (0, pair))
+    own = pl.BlockSpec((slot_len, LANES), lambda i, n: (0, 0))
+    before = () if before is None else tuple(before)
+    both = pltpu.VMEM((2, slot_len, LANES), BF16)
+    wide = PARTS * LANES
+    return pl.pallas_call(
+        attend_back_kernel,
+        out_shape=(
+            jax.ShapeDtypeStruct((slot_len, cols), F32),
+            jax.ShapeDtypeStruct((slot_len, PARTS * cols), BF16),
+            jax.ShapeDtypeStruct((slot_len // 2, wide), BF16),
+        ),
+        grid_spec=pltpu.PrefetchScalarGridSpec(
+            num_scalar_prefetch=1,
+            grid=(1,),
+            in_specs=[full, full, full, own, full, full, own, own]
+            + [pl.BlockSpec(memory_space=pl.ANY) for _ in before],
+            out_specs=[
+                full,
+                pl.BlockSpec((slot_len, wide), lambda i, n: (0, pair)),
+                pl.BlockSpec((slot_len // 2, wide), lambda i, n: (0, 0)),
+            ],
+            scratch_shapes=[both] * 7
+            + [pltpu.VMEM((BLK, BLK), F32), pltpu.VMEM((slot_len, LANES), F32)],
+        ),
+        input_output_aliases={9 + n: n for n in range(len(before))},
+        compiler_params=params(VMEM_MIB),
+        cost_estimate=cost(5 * 2 * slot_len * slot_len * 256, 6e6),
+        name="attend_back_pair",
+    )(length, q, k, v, do, o, lse, cosine, sine, *before)
+
+
+def resid_kernel(base_ref, x_ref, gain_ref, w_own_ref, w_far_ref, own_ref, *refs):
+    own = own_ref[...]
+    far = jnp.concatenate([r[...] for r in refs[:-3]], axis=1)
+    h_ref, n_ref, o_ref = refs[-3:]
+    h = x_ref[...].astype(F32) + (nn(own, w_own_ref[...]) + nn(far, w_far_ref[...]))
+    inverse = lax.rsqrt(jnp.mean(h * h, axis=-1, keepdims=True) + EPS)
+    h_ref[...] = h
+    n_ref[...] = ((h * inverse) * gain_ref[...]).astype(BF16)
+    cols = own.shape[1]
+    o_ref[:, :cols] = far
+    o_ref[:, cols:] = own
+
+
+def resid_rows(base, x, gain, w_own, w_far, own, far):
+    rows, model = x.shape
+    cols = w_own.shape[0]
+    wide = pl.BlockSpec((BLK, model), lambda i, b: (i, 0))
+    fixed = pl.BlockSpec((cols, model), lambda i, b: (0, 0))
+    return pl.pallas_call(
+        resid_kernel,
+        out_shape=(
+            jax.ShapeDtypeStruct((rows, model), F32),
+            jax.ShapeDtypeStruct((rows, model), BF16),
+            jax.ShapeDtypeStruct((rows, 2 * cols), BF16),
+        ),
+        grid_spec=pltpu.PrefetchScalarGridSpec(
+            num_scalar_prefetch=1,
+            grid=(rows // BLK,),
+            in_specs=[
+                wide,
+                pl.BlockSpec((1, model), lambda i, b: (0, 0)),
+                fixed,
+                fixed,
+                pl.BlockSpec((BLK, cols), lambda i, b: (b[0] + i, 0)),
+                *(pl.BlockSpec((BLK, f.shape[1]), lambda i, b: (i, 0)) for f in far),
+            ],
+            out_specs=[wide, wide, pl.BlockSpec((BLK, 2 * cols), lambda i, b: (i, 0))],
+        ),
+        compiler_params=params(VMEM_MIB),
+        cost_estimate=cost(2 * rows * model * cols * 2, 14e6),
+        name="resid_rows",
+    )(base, x, gain, w_own, w_far, own, *far)
+
+
+def interleave_kernel(w_ref, out_ref):
+    for run in range(w_ref.shape[2] // LANES):
+        for side in (0, 1):
+            spot = (2 * run + side) * LANES
+            out_ref[:, spot : spot + LANES] = w_ref[:, side, run * LANES : (run + 1) * LANES].astype(BF16)
+
+
+def interleave(w):
+    model, sides, hidden = w.shape
+    return pl.pallas_call(
+        interleave_kernel,
+        out_shape=jax.ShapeDtypeStruct((model, sides * hidden), BF16),
+        grid=(model // 128,),
+        in_specs=[pl.BlockSpec((128, sides, hidden), lambda i: (i, 0, 0))],
+        out_specs=pl.BlockSpec((128, sides * hidden), lambda i: (i, 0)),
+        compiler_params=params(VMEM_MIB),
+        cost_estimate=cost(0, 6 * w.size),
+        name="interleave",
+    )(w)
+
+
+def halve_rows(grad, core, x, keep, send):
+    rows = grad.shape[0] // 16
+    block = lambda z, i, c: grad[(z * 4 + i * 2 + c) * rows : (z * 4 + i * 2 + c + 1) * rows]
+    for i in (0, 1):
+        for z in range(4):
+            spot = pl.ds((i * 4 + z) * rows, rows)
+            same = [jnp.where(x == 0, block(z, i, c), block(z, 1 - i, c)) for c in (0, 1)]
+            keep[spot, :] = jnp.where(core == 0, same[0], same[1])
+            send[spot, :] = jnp.where(core == 0, same[1], same[0])
+
+
+def runs(block, count, of, which):
+    return jnp.concatenate(
+        [block[:, (of * i + which) * LANES : (of * i + which + 1) * LANES] for i in range(count)], axis=1
+    )
+
+
+def swiglu_kernel(place_ref, n_ref, dy_ref, wgu_ref, wd_ref, y_ref, dn_ref, keep_ref, send_ref, y_acc, dn_acc):
+    step = pl.program_id(0)
+    last = pl.num_programs(0) - 1
+    core, x = place_ref[0], place_ref[1]
+
+    def work(count, first):
+        n = n_ref[...]
+        dy = dy_ref[...]
+        wgu, wd = wgu_ref[:, : 2 * count * LANES], wd_ref[: count * LANES, :]
+        both = nn(n, wgu)
+        gate, up = runs(both, count, 2, 0), runs(both, count, 2, 1)
+        sig = jax.nn.sigmoid(gate)
+        silu = gate * sig
+        hid = (silu * up).astype(BF16)
+        dhid = nt(dy, wd)
+        dgate = (dhid * up * sig * (1.0 + gate * (1.0 - sig))).astype(BF16)
+        dup = (dhid * silu).astype(BF16)
+        dgu = jnp.concatenate(
+            [d[:, i * LANES : (i + 1) * LANES] for i in range(count) for d in (dgate, dup)], axis=1
+        )
+        y = nn(hid, wd)
+        dn = nt(dgu, wgu)
+        if first:
+            y_acc[...] = y
+            dn_acc[...] = dn
+        else:
+            y_acc[...] += y
+            dn_acc[...] += dn
+        grad_gu = tn(n, dgu).astype(BF16)
+        grad_d = tn(dy, hid).astype(BF16)
+        for i in range(count):
+            for part, grad in enumerate((grad_gu[:, 2 * i * LANES : (2 * i + 2) * LANES],
+                                         grad_d[:, i * LANES : (i + 1) * LANES])):
+                spot = slice((3 * i + 2 * part) * LANES, (3 * i + 2 * part) * LANES + grad.shape[1])
+                halve_rows(grad, core, x, keep_ref.at[:, spot], send_ref.at[:, spot])
+
+    @pl.when(step == 0)
+    def _():
+        work(2, True)
+
+    @pl.when((step > 0) & (step < last))
+    def _():
+        work(2, False)
+
+    @pl.when(step == last)
+    def _():
+        work(1, False)
+        y_ref[...] = y_acc[...].astype(BF16)
+        dn_ref[...] = dn_acc[...].astype(BF16)
+
+
+def swiglu_half(place, n, dy, wgu, wd, width):
+    rows, model = n.shape
+    hidden = wd.shape[0]
+    tile = 256
+    steps = -(-hidden // tile)
+    held = pl.BlockSpec((rows, model), lambda t, p: (0, 0))
+    grads = pl.BlockSpec((model // 2, 3 * tile), lambda t, p: (0, t))
+    return pl.pallas_call(
+        swiglu_kernel,
+        out_shape=(
+            *(jax.ShapeDtypeStruct((rows, model), BF16) for _ in range(2)),
+            *(jax.ShapeDtypeStruct((model // 2, width), BF16) for _ in range(2)),
+        ),
+        grid_spec=pltpu.PrefetchScalarGridSpec(
+            num_scalar_prefetch=1,
+            grid=(steps,),
+            in_specs=[
+                held,
+                held,
+                pl.BlockSpec((model, 2 * tile), lambda t, p: (0, t)),
+                pl.BlockSpec((tile, model), lambda t, p: (t, 0)),
+            ],
+            out_specs=[held, held, grads, grads],
+            scratch_shapes=[pltpu.VMEM((rows, model), F32)] * 2,
+        ),
+        compiler_params=params(VMEM_MIB),
+        cost_estimate=cost(9 * 2 * rows * model * hidden, 36e6, rows * hidden),
+        name="swiglu_half",
+    )(place, n, dy, wgu, wd)
+
+
+def grad_out_kernel(place_ref, dhb_ref, o_ref, keep_in, send_in, keep_ref, send_ref):
+    del keep_in, send_in
+    grad = tn(dhb_ref[...], o_ref[...]).astype(BF16)
+    halve_rows(grad, place_ref[0], place_ref[1], keep_ref, send_ref)
+
+
+def grad_out_into(place, dhb, o_cat, keep, send, start):
+    rows, model = dhb.shape
+    tile = 384
+    out = pl.BlockSpec((model // 2, tile), lambda t, p: (0, start // tile + t))
+    return pl.pallas_call(
+        grad_out_kernel,
+        out_shape=[jax.ShapeDtypeStruct(a.shape, a.dtype) for a in (keep, send)],
+        grid_spec=pltpu.PrefetchScalarGridSpec(
+            num_scalar_prefetch=1,
+            grid=(-(-o_cat.shape[1] // tile),),
+            in_specs=[
+                pl.BlockSpec((rows, model), lambda t, p: (0, 0)),
+                pl.BlockSpec((rows, tile), lambda t, p: (0, t)),
+                pl.BlockSpec(memory_space=pl.ANY),
+                pl.BlockSpec(memory_space=pl.ANY),
+            ],
+            out_specs=[out, out],
+        ),
+        input_output_aliases={3: 0, 4: 1},
+        compiler_params=params(VMEM_MIB),
+        cost_estimate=cost(2 * rows * model * o_cat.shape[1], 7e6),
+        name="grad_out",
+    )(place, dhb, o_cat, keep, send)
+
+
+def grad_qkv_kernel(place_ref, n_ref, dqkv_ref, w_ref, keep_ref, send_ref, t_ref):
+    grad = tn(n_ref[...], dqkv_ref[...])
+    term = None
+    for part in range(PARTS):
+        piece = grad[:, part * LANES : (part + 1) * LANES] * w_ref[part].astype(F32)
+        term = piece if term is None else term + piece
+
+    @pl.when(pl.program_id(0) == 0)
+    def _():
+        t_ref[...] = term
+
+    @pl.when(pl.program_id(0) > 0)
+    def _():
+        t_ref[...] += term
+
+    halve_rows(grad.astype(BF16), place_ref[0], place_ref[1], keep_ref, send_ref)
+
+
+def grad_qkv_of(place, norm, dqkv, w):
+    slot_len, model = norm.shape
+    tile = PARTS * LANES
+    out = pl.BlockSpec((model // 2, tile), lambda t, p: (0, t))
+    return pl.pallas_call(
+        grad_qkv_kernel,
+        out_shape=(
+            *(jax.ShapeDtypeStruct((model // 2, dqkv.shape[1]), BF16) for _ in range(2)),
+            jax.ShapeDtypeStruct((model, LANES), F32),
+        ),
+        grid_spec=pltpu.PrefetchScalarGridSpec(
+            num_scalar_prefetch=1,
+            grid=(dqkv.shape[1] // tile,),
+            in_specs=[
+                pl.BlockSpec((slot_len, model), lambda t, p: (0, 0)),
+                pl.BlockSpec((slot_len, tile), lambda t, p: (0, t)),
+                pl.BlockSpec((PARTS, model, LANES), lambda t, p: (0, 0, t)),
+            ],
+            out_specs=[out, out, pl.BlockSpec((model, LANES), lambda t, p: (0, 0))],
+        ),
+        compiler_params=params(VMEM_MIB),
+        cost_estimate=cost(2 * slot_len * model * dqkv.shape[1], 14e6),
+        name="grad_qkv",
+    )(place, norm, dqkv, w)
+
+
+def after_kernel(h_ref, y1_ref, y2_ref, d1_ref, d2_ref, dy_ref, gain_ref, w_own_ref, w_far_ref,
+                 out_ref, dh_ref, dhb_ref, own_ref, far_ref, t_ref):
+    h = h_ref[...]
+    out_ref[...] = (h + (y1_ref[...].astype(F32) + y2_ref[...].astype(F32))).astype(BF16)
+    inverse = lax.rsqrt(jnp.mean(h * h, axis=-1, keepdims=True) + EPS)
+    unit = h * inverse
+    dn = d1_ref[...].astype(F32) + d2_ref[...].astype(F32)
+    e = dn * gain_ref[...]
+    dh = dy_ref[...].astype(F32) + inverse * (e - unit * jnp.mean(e * unit, axis=-1, keepdims=True))
+    dh_ref[...] = dh
+    dhb = dh.astype(BF16)
+    dhb_ref[...] = dhb
+    own_ref[...] = nt(dhb, w_own_ref[...]).astype(BF16)
+    far_ref[...] = nt(dhb, w_far_ref[...]).astype(BF16)
+
+    @pl.when(pl.program_id(0) == 0)
+    def _():
+        t_ref[...] = jnp.zeros_like(t_ref)
+
+    t_ref[...] += jnp.sum(dn * unit, axis=0, keepdims=True)
+
+
+def after_rows(h, y1, y2, d1, d2, dy, gain, w_own, w_far):
+    rows, model = h.shape
+    cols = w_own.shape[0]
+    wide = pl.BlockSpec((BLK, model), lambda i: (i, 0))
+    fixed = pl.BlockSpec((cols, model), lambda i: (0, 0))
+    slim = pl.BlockSpec((BLK, cols), lambda i: (i, 0))
+    one = pl.BlockSpec((1, model), lambda i: (0, 0))
+    return pl.pallas_call(
+        after_kernel,
+        out_shape=(
+            jax.ShapeDtypeStruct((rows, model), BF16),
+            jax.ShapeDtypeStruct((rows, model), F32),
+            jax.ShapeDtypeStruct((rows, model), BF16),
+            jax.ShapeDtypeStruct((rows, cols), BF16),
+            jax.ShapeDtypeStruct((rows, cols), BF16),
+            jax.ShapeDtypeStruct((1, model), F32),
+        ),
+        grid=(rows // BLK,),
+        in_specs=[wide] * 6 + [one, fixed, fixed],
+        out_specs=[wide, wide, wide, slim, slim, one],
+        compiler_params=params(VMEM_MIB),
+        cost_estimate=cost(2 * rows * model * cols * 2, 36e6),
+        name="after_rows",
+    )(h, y1, y2, d1, d2, dy, gain, w_own, w_far)
+
+
+def input_kernel(base_ref, x_ref, dh_ref, gain_ref, w_own_ref, w_far_ref, *refs):
+    out_ref = refs[-1]
+    dn = None
+    for weights, grads in ((w_own_ref, refs[:1]), (w_far_ref, refs[1:-1])):
+        flat = jnp.concatenate([g[...] for g in grads], axis=1)
+        for part in range(PARTS):
+            term = nt(runs(flat, flat.shape[1] // (PARTS * LANES), PARTS, part), weights[part])
+            dn = term if dn is None else dn + term
+    x = x_ref[...].astype(F32)
+    inverse = lax.rsqrt(jnp.mean(x * x, axis=-1, keepdims=True) + EPS)
+    unit = x * inverse
+    e = dn * gain_ref[...]
+    out_ref[...] = dh_ref[...] + inverse * (e - unit * jnp.mean(e * unit, axis=-1, keepdims=True))
+
+
+def input_rows(base, x, dh, gain, w_own, w_far, own, far):
+    rows, model = x.shape
+    cols = w_own.shape[2]
+    wide = pl.BlockSpec((BLK, model), lambda i, b: (i, 0))
+    fixed = pl.BlockSpec((PARTS, model, cols), lambda i, b: (0, 0, 0))
+    return pl.pallas_call(
+        input_kernel,
+        out_shape=jax.ShapeDtypeStruct((rows, model), F32),
+        grid_spec=pltpu.PrefetchScalarGridSpec(
+            num_scalar_prefetch=1,
+            grid=(rows // BLK,),
+            in_specs=[wide, wide, pl.BlockSpec((1, model), lambda i, b: (0, 0)), fixed, fixed]
+            + [pl.BlockSpec((BLK, own.shape[1]), lambda i, b: (b[0] + i, 0))]
+            + [pl.BlockSpec((BLK, f.shape[1]), lambda i, b: (i, 0)) for f in far],
+            out_specs=wide,
+        ),
+        compiler_params=params(VMEM_MIB),
+        cost_estimate=cost(2 * rows * model * cols * 6, 20e6),
+        name="input_rows",
+    )(base, x, dh, gain, w_own, w_far, own, *far)
+
+
+def step_of(sum_grad, weight, moment, average, rate, root_count):
+    return nesterov(sum_grad / root_count, weight, moment, average, rate)
+
+
+def own_columns(place, wide):
+    turned = wide.T
+    half = turned.shape[0] // 2
+    return jnp.where(place == 0, turned[:half], turned[half:])
+
+
+def step_mlp_kernel(root_count, place_ref, sum_ref, got_ref, wgu_ref, mgu_ref, agu_ref, wd_ref, md_ref, ad_ref, *outs):
+    total = sum_ref[...] + got_ref[...].astype(F32)
+    count = total.shape[1] // (3 * LANES)
+    for side in (0, 1):
+        grads = step_of(runs(total, count, 3, side), wgu_ref[:, side, :], mgu_ref[:, side, :],
+                        agu_ref[:, side, :], RATE_GATEUP, root_count)
+        for out, value in zip(outs[:4], grads):
+            out[:, side, :] = value
+    weight = own_columns(place_ref[1], wd_ref[...])
+    grads = step_of(runs(total, count, 3, 2), weight, md_ref[...], ad_ref[...], RATE_DOWN, root_count)
+    for out, value in zip(outs[4:], grads):
+        out[...] = value
+
+
+def step_mlp(dp_index, root_count, total, got, w_gateup, m_gu, a_gu, w_down, m_d, a_d):
+    place = jnp.stack([dp_index, dp_index % 2, dp_index // 2]).astype(jnp.int32)
+    share, sides, hidden = m_gu.shape
+    cols = total.shape[1]
+    gu = pl.BlockSpec((share, sides, hidden), lambda i, p: (0, 0, 0))
+    d = pl.BlockSpec((share, hidden), lambda i, p: (0, 0))
+    return pl.pallas_call(
+        functools.partial(step_mlp_kernel, root_count),
+        out_shape=(
+            *(jax.ShapeDtypeStruct(m_gu.shape, F32) for _ in range(4)),
+            *(jax.ShapeDtypeStruct((share, hidden), F32) for _ in range(4)),
+        ),
+        grid_spec=pltpu.PrefetchScalarGridSpec(
+            num_scalar_prefetch=1,
+            grid=(1,),
+            in_specs=[
+                pl.BlockSpec((share, cols), lambda i, p: (0, 0)),
+                pl.BlockSpec((share, cols), lambda i, p: (0, 0)),
+                pl.BlockSpec((share, sides, hidden), lambda i, p: (p[0], 0, 0)),
+                gu,
+                gu,
+                pl.BlockSpec((hidden, LANES), lambda i, p: (0, p[2])),
+                d,
+                d,
+            ],
+            out_specs=[gu] * 4 + [d] * 4,
+        ),
+        compiler_params=params(VMEM_MIB),
+        cost_estimate=cost(0, 14e6),
+        name="step_mlp",
+    )(place, total, got, w_gateup, m_gu, a_gu, w_down, m_d, a_d)
+
+
+def step_attention_kernel(root_count, place_ref, sum_ref, own_ref, got_ref, wq_ref, mq_ref, aq_ref, wo_ref, mo_ref, ao_ref, *outs):
+    total = sum_ref[...]
+    count = total.shape[1] // (PARTS * LANES)
+    for part in range(PARTS):
+        grads = step_of(runs(total, count, PARTS, part), wq_ref[part], mq_ref[part], aq_ref[part],
+                        RATE_QKV, root_count)
+        for out, value in zip(outs[:4], grads):
+            out[part] = value
+    weight = own_columns(place_ref[1], wo_ref[...])
+    grads = step_of(own_ref[...] + got_ref[...].astype(F32), weight, mo_ref[...], ao_ref[...],
+                    RATE_OUT, root_count)
+    for out, value in zip(outs[4:], grads):
+        out[...] = value
+
+
+def step_attention(dp_index, root_count, total, own, got, w_qkv, m_q, a_q, w_out, m_o, a_o):
+    place = jnp.stack([dp_index, dp_index % 2, dp_index // 2]).astype(jnp.int32)
+    parts, share, cols = m_q.shape
+    q = pl.BlockSpec((parts, share, cols), lambda i, p: (0, 0, 0))
+    o = pl.BlockSpec((share, cols), lambda i, p: (0, 0))
+    return pl.pallas_call(
+        functools.partial(step_attention_kernel, root_count),
+        out_shape=(
+            *(jax.ShapeDtypeStruct(m_q.shape, F32) for _ in range(4)),
+            *(jax.ShapeDtypeStruct((share, cols), F32) for _ in range(4)),
+        ),
+        grid_spec=pltpu.PrefetchScalarGridSpec(
+            num_scalar_prefetch=1,
+            grid=(1,),
+            in_specs=[
+                pl.BlockSpec((share, parts * cols), lambda i, p: (0, 0)),
+                o,
+                o,
+                pl.BlockSpec((parts, share, cols), lambda i, p: (0, p[0], 0)),
+                q,
+                q,
+                pl.BlockSpec((cols, LANES), lambda i, p: (0, p[2])),
+                o,
+                o,
+            ],
+            out_specs=[q] * 4 + [o] * 4,
+        ),
+        compiler_params=params(VMEM_MIB),
+        cost_estimate=cost(0, 6e6),
+        name="step_attention",
+    )(place, total, own, got, w_qkv, m_q, a_q, w_out, m_o, a_o)
+
+
+def dp_pairs(move):
+    return tuple((i, move(i)) for i in range(16))
+
+
+CORE = dp_pairs(lambda i: i ^ 1)
+CROSS = dp_pairs(lambda i: i ^ 2)
+NEAR = tuple(
+    tuple((i, i ^ flip) for i in range(32)) for flip in (1, 2, 3)
+)
+ALONG = tuple(dp_pairs(lambda i, step=step: (i + 4 * step) % 16) for step in (1, 2, 3))
+
+
+def move(x, pairs):
+    return lax.ppermute(x, "dp", pairs)
+
+
+def add(left, right):
+    return left.astype(F32) + right.astype(F32)
+
+
+def after_core(keep, got):
+    half = keep.shape[0] // 2
+    here = add(keep[:half], got[:half]).astype(BF16)
+    away = add(keep[half:], got[half:]).astype(BF16)
+    return here, away
+
+
+def after_cross(here, got, z):
+    total = add(here, got)
+    rows = here.shape[0] // 4
+    block = lambda step: lax.dynamic_slice_in_dim(total, lax.rem(z + step, 4) * rows, rows, 0)
+    return block(0), tuple(block(step).astype(BF16) for step in (1, 2, 3))
+
+
+def after_along(mine, got):
+    for piece in got:
+        mine = mine + piece.astype(F32)
+    return mine
+
+
+def tie(values, *others):
+    return lax.optimization_barrier((values, others))[0]
+
+
+def shards_pair(
+    tokens,
+    first_values,
+    lengths,
+    cotangent,
+    w_qkv,
+    w_out,
+    w_gateup,
+    w_down,
+    gains,
+    moment_qkv,
+    moment_out,
+    moment_gateup,
+    moment_down,
+    moment_gains,
+    average_qkv,
+    average_out,
+    average_gateup,
+    average_down,
+    average_gains,
+):
+    rows, model = tokens.shape
+    mp_index = lax.axis_index("mp")
+    dp_index = lax.axis_index("dp")
+    dp_count = lax.axis_size("dp")
+    z, core = dp_index // 4, dp_index % 2
+    place = jnp.stack([core, (dp_index // 2) % 2]).astype(jnp.int32)
+    slot_len = 2 * rows
+    head_cols = w_qkv.shape[2]
+    hidden = w_gateup.shape[2]
+    pairs = head_cols // LANES
+    root_count = math.sqrt(slot_len * dp_count)
+    row_start = mp_index * rows
+    far_start = (1 - mp_index) * rows
+    gain_one, gain_two = gains[0:1], gains[1:2]
+
+    def swap(x):
+        return lax.ppermute(x, "mp", SWAP)
+
+    def chunk(x):
+        part = x.shape[0] // dp_count
+        return lax.dynamic_slice_in_dim(x, dp_index * part, part, 0)
+
+    def gather(x):
+        return lax.all_gather(x, "dp", axis=0, tiled=True)
+
+    out_bf = w_out.astype(BF16)
+    out_chunk = swap(chunk(w_out).astype(BF16))
+    far_tokens = swap(tie(tokens, out_chunk))
+    out_far = gather(out_chunk)
+    qkv_bf = w_qkv.transpose(1, 0, 2).astype(BF16)
+    gateup_bf = interleave(w_gateup)
+    down_bf = w_down.astype(BF16)
+    cosine, sine = pair_tables(slot_len)
+    block_of = lambda start: (start // BLK).astype(jnp.int32)
+    base, far_base = block_of(row_start).reshape(1), block_of(far_start).reshape(1)
+    own_part = project_qkv(base, tokens, first_values, gain_one, qkv_bf, cosine, sine, None)
+    place_row = row_start + jnp.arange(rows, dtype=jnp.int32)
+    dy = jnp.where((place_row < lengths[0])[:, None], cotangent, jnp.zeros_like(cotangent))
+    far_tokens, own_part, gateup_bf, down_bf, dy, out_far = lax.optimization_barrier(
+        (far_tokens, own_part, gateup_bf, down_bf, dy, out_far)
+    )
+    gateup_chunk = swap(chunk(gateup_bf))
+    down_chunk = swap(tie(chunk(down_bf), gateup_chunk))
+    qkv_chunk = swap(tie(chunk(qkv_bf.reshape(PARTS * model, head_cols)), down_chunk))
+
+    norm_one, q, k, v = project_qkv(
+        far_base, far_tokens, first_values, gain_one, qkv_bf, cosine, sine, own_part
+    )
+    q, gateup_chunk, down_chunk, qkv_chunk = lax.optimization_barrier(
+        (q, gateup_chunk, down_chunk, qkv_chunk)
+    )
+    gateup_far = gather(gateup_chunk)
+    down_far = gather(tie(down_chunk, gateup_far))
+    qkv_far = gather(tie(qkv_chunk, down_far)).reshape(PARTS, model, head_cols)
+
+    mixed = None
+    o_far = []
+    for pair in range(pairs):
+        lanes = slice(pair * LANES, (pair + 1) * LANES)
+        mixed = attend_pair(pair, lengths, q, k, v, mixed)
+        if pair == pairs - 2:
+            piece = lax.dynamic_slice_in_dim(mixed[0][:, : lanes.stop], far_start, rows, 0)
+            piece, mixed = lax.optimization_barrier((piece, mixed))
+            o_far.append(swap(piece))
+        if pair == pairs - 1:
+            o_far.append(swap(lax.dynamic_slice_in_dim(mixed[0][:, lanes], far_start, rows, 0)))
+    o_all, lse_all = mixed
+    h, norm_two, o_cat = resid_rows(base, tokens, gain_two, out_bf, out_far, o_all, o_far)
+
+    runs_width = 3 * hidden
+    norm_two, gateup_far = lax.optimization_barrier((norm_two, gateup_far))
+    y_own, dn_own, keep_own, send_own = swiglu_half(place, norm_two, dy, gateup_bf, down_bf, runs_width)
+    got_own = move(send_own, CORE)
+    far_width = runs_width + 3 * 384
+    (norm_two, gateup_far, down_far) = tie((norm_two, gateup_far, down_far), y_own)
+    y_far, dn_far, keep_far, send_far = swiglu_half(place, norm_two, dy, gateup_far, down_far, far_width)
+    here_own, away_own = after_core(keep_own, tie(got_own, y_far))
+    got_own = move(away_own, CROSS)
+    y_far = tie(y_far, away_own)
+    output, dh, dhb, do_own, do_far, gain_two_part = after_rows(
+        h, y_own, y_far, dn_own, dn_far, dy, gain_two, out_bf, out_far
+    )
+    theirs = [swap(do_far[:, :LANES]), swap(do_far[:, LANES:])]
+    keep_far, send_far = grad_out_into(place, dhb, o_cat, keep_far, send_far, runs_width)
+    got_far = move(send_far, CORE)
+
+    theirs, qkv_far = lax.optimization_barrier((theirs, qkv_far))
+    back = None
+    dqkv_far = []
+    far_place = jnp.concatenate([lengths, far_base])
+    for pair in range(pairs):
+        lanes = slice(pair * LANES, (pair + 1) * LANES)
+        mine = do_own[:, lanes]
+        other = theirs[0] if pair == 0 else theirs[1][:, (pair - 1) * LANES : pair * LANES]
+        if pair == 1:
+            here_far, away_far = after_core(keep_far, tie(got_far, back))
+            got_far = move(away_far, CROSS)
+            other = tie(other, away_far)
+        if pair == 2:
+            mine_own, blocks_own = after_cross(here_own, tie(got_own, back), z)
+            got_own = tuple(move(b, p) for b, p in zip(blocks_own, ALONG))
+            other, dqkv_far[0] = lax.optimization_barrier((tie(other, blocks_own, mine_own), dqkv_far[0]))
+        if pair == 3:
+            mine_far, blocks_far = after_cross(here_far, tie(got_far, back), z)
+            got_far = tuple(move(b, p) for b, p in zip(blocks_far, ALONG))
+            other, dqkv_far[1] = lax.optimization_barrier((tie(other, blocks_far, mine_far), dqkv_far[1]))
+        low = jnp.where(mp_index == 0, mine, other)
+        high = jnp.where(mp_index == 0, other, mine)
+        do = jnp.concatenate([low, high], axis=0)
+        first_grad, dqkv, away = attend_back_pair(
+            pair, far_place, q, k, v, do, o_all, lse_all, cosine, sine, back
+        )
+        back = (first_grad, dqkv)
+        dqkv_far.append(swap(away))
+
+    dqkv, dqkv_far[2], got_own = lax.optimization_barrier((dqkv, dqkv_far[2], got_own))
+    sum_own = after_along(mine_own, got_own)
+    keep_qkv, send_qkv, gain_one_lanes = grad_qkv_of(place, norm_one, dqkv, qkv_bf)
+    got_qkv = move(send_qkv, CORE)
+    gain_one_part = jnp.sum(gain_one_lanes, axis=1) / gains[0]
+    parts = jnp.stack([gain_one_part, gain_two_part[0]], axis=0)
+    near = [lax.ppermute(parts, ("dp", "mp"), p) for p in NEAR]
+    got_qkv, near = lax.optimization_barrier((got_qkv, near))
+    here_qkv, away_qkv = after_core(keep_qkv, got_qkv)
+    got_qkv = move(away_qkv, CROSS)
+    parts = after_along(parts, near)
+    cross = move(parts, CROSS)
+    input_grad = input_rows(
+        base, tokens, tie(dh, away_qkv, parts), gain_one, qkv_bf, qkv_far, dqkv, dqkv_far
+    )
+    got_qkv, cross, got_far = tie((got_qkv, cross, got_far), input_grad)
+    mine_qkv, blocks_qkv = after_cross(here_qkv, got_qkv, z)
+    got_qkv = tuple(move(b, p) for b, p in zip(blocks_qkv, ALONG))
+    parts = parts + cross
+    along = [move(parts, p) for p in ALONG]
+    sum_far = after_along(mine_far, got_far)
+    cut = runs_width + head_cols
+    got_swap = swap(sum_far[:, :cut].astype(BF16))
+
+    gateup_down = step_mlp(
+        dp_index, root_count, tie(sum_own, blocks_qkv, parts), got_swap[:, :runs_width], w_gateup,
+        moment_gateup, average_gateup, w_down, moment_down.T, average_down.T,
+    )
+    got_qkv, along = tie((got_qkv, along), gateup_down[0])
+    gain_sum = after_along(parts, along)
+    sum_qkv = after_along(mine_qkv, got_qkv)
+    turn = lambda x: x.transpose(1, 0, 2)
+    qkv_out = step_attention(
+        dp_index, root_count, sum_qkv, sum_far[:, cut : cut + head_cols], got_swap[:, runs_width:],
+        turn(w_qkv), turn(moment_qkv), turn(average_qkv), w_out, moment_out.T, average_out.T,
+    )
+    gains_set = nesterov(gain_sum / root_count, gains, moment_gains, average_gains, RATE_GAINS)
+    return (
+        output,
+        input_grad,
+        first_grad,
+        *(turn(x) for x in qkv_out[:4]),
+        *(x.T for x in qkv_out[4:]),
+        *gateup_down[:4],
+        *(x.T for x in gateup_down[4:]),
+        *gains_set,
+    )
+
+
 def solution(mesh):
     placed = (
         P(("dp", "mp"), None),
@@ -370,7 +1319,7 @@
         P(),
     )
     return jax.shard_map(
-        shards,
+        shards_pair if (mesh.shape["dp"], mesh.shape["mp"]) == (16, 2) else shards_any,
         mesh=mesh,
         in_specs=placed,
         out_specs=(

time: 1630 us -> 598 us (0.37)
  matrix products: 582 us -> 0 us
  waiting for transfers between devices: 521 us -> 141 us
  Pallas kernels: 0 us -> 330 us
  other arithmetic: 269 us -> 47.4 us
  local copies, waits for them, and re-layouts: 184 us -> 20.3 us
  blocking collectives: 39.9 us -> 0 us
  starting transfers between devices: 0.9 us -> 34.2 us
    dot_general x40 -> x0, matrix products: 582 us -> none  [the longest x8 158 us: block_scores(): jnp.einsum('qhd,khd->hqk', query_block, keys, preferred_element_type=jnp....]
    reduce_scatter x7 -> x0, waiting for transfers between devices: 377 us -> none  [the longest x1 99.3 us: shards(): lax.psum_scatter(dot_last(grad_gateup_bf, gateup_bf), 'mp', scatter_dimen...]
    pallas_call x0 -> x20, Pallas kernels: none -> 330 us  [the longest x4 106 us: attend_back_pair(): pl.pallas_call(attend_back_kernel, out_shape=(jax.ShapeDtypeStruct((slot_...]
    convert_element_type x11 -> x6, other arithmetic: 130 us -> 16.5 us  [the longest x3 10.2 us: after_core(): away = add(keep[half:], got[half:]).astype(BF16)]
    all_gather x4, waiting for transfers between devices: 143 us -> 38 us  [gather(): return lax.all_gather(x, 'dp', axis=0, tiled=True)]
    ppermute x0 -> x36, waiting for transfers between devices: none -> 103 us  [the longest x14 73.1 us: swap(): return lax.ppermute(x, 'mp', SWAP)]
    dynamic_update_slice x8 -> x0, local copies, waits for them, and re-layouts: 92.9 us -> none  [per_slot(): lax.map(per_block, (slot_queries.reshape(blocks, block_len, heads_here, h...]
    reduce_sum x8 -> x1, other arithmetic: 75.1 us -> 1.25 us  [shards_pair(): gain_one_part = jnp.sum(gain_one_lanes, axis=1) / gains[0]]
  transfers between devices with their start and end apart: 12 -> 40, of which waited for: 9 -> 10; matrix products, arithmetic and copies ran while one was open for 45% -> 10% of each run, Pallas kernels for 0% -> 53%
where the time goes in v1:
time: 598 us; the launch traced here: 588 us
  Pallas kernels  330 us (55%)
  waiting for transfers between devices  141 us (24%)
  other arithmetic  47.4 us (8%)
  starting transfers between devices  34.2 us (6%)
  local copies, waits for them, and re-layouts  20.3 us (3%)
  between operations  15.1 us (3%)
    pallas_call x4, Pallas kernels, attend_back_pair(): pl.pallas_call(attend_back_kernel, out_shape=(jax.ShapeDtypeStruct((slot_...  106 us
    ppermute x14, waiting for transfers between devices, swap(): return lax.ppermute(x, 'mp', SWAP)  73.1 us
    pallas_call x2, Pallas kernels, swiglu_half(): pl.pallas_call(swiglu_kernel, out_shape=(*(jax.ShapeDtypeStruct((rows, mo...  71.8 us
    pallas_call x4, Pallas kernels, attend_pair(): pl.pallas_call(attend_fwd_kernel, out_shape=(jax.ShapeDtypeStruct((slot_l...  52.4 us
    all_gather x4, waiting for transfers between devices, gather(): return lax.all_gather(x, 'dp', axis=0, tiled=True)  38 us
    ppermute x19, waiting for transfers between devices, move(): return lax.ppermute(x, 'dp', pairs)  29.6 us
    ppermute x19, starting transfers between devices, move(): return lax.ppermute(x, 'dp', pairs)  17.7 us
    pallas_call x2, Pallas kernels, project_qkv(): pl.pallas_call(qkv_kernel, out_shape=outs, grid_spec=pltpu.PrefetchScalar...  16.8 us
  transfers between devices with their start and end apart: 40, of which 10 were waited for; matrix products, arithmetic and copies ran while one was open for 10% of the time, Pallas kernels for 53%

profile of v1, /device:TPU:0, one launch (start us, length us, event | category | flops | bytes accessed | tf_op | source)
XLA Modules:
  0.0 587.7 jit_solution(16432080143546244600)
XLA Ops:
  16.3 15.5 %interleave.1.wgu_ref = bf16[1024,2816]{1,0:T(8,128)(2,1)} custom-call(f32[1024,2,1408]{2,1,0:T(2,128)} %wgu_ref.1), custom_call_target="tpu_custom_call" | custom-call | bytes 17301504 | tf_op jit(solution)/shard_map/interleave/pallas_call | solution.py:694
  32.6 3.9 fusion.2
  41.6 8.4 %project_qkv.2 = (bf16[2048,1024]{1,0:T(8,128)(2,1)}, bf16[2048,512]{1,0:T(8,128)(2,1)}, bf16[2048,512]{1,0:T(8,128)(2,1)}, bf16[2048,512]{1,0:T(8,128)(2,1)}) custom-call(s32[1]{0:T(128)} %bitcast.base_ref, bf16[1024,1024]{1,0:T(8,128)(2,1)} %x_ref.5, bf16[2048,512]{1,0:T(8,128)(2,1)} %first_ref.3, f32[1,1024]{1,0:T(1,128)} %get-tuple-element.305.gain_ref, ...), custom_call_target="tpu_custom_call" | custom-call | flops 3221225472 | bytes 10000000 | tf_op jit(solution)/shard_map/project_qkv/pallas_call | solution.py:427
  53.2 18.5 %all-gather.5.cloned.1.call-done.w_far_ref = bf16[512,1024]{1,0:T(8,128)(2,1)} async-done(((bf16[32,1024]{1,0:T(8,128)(2,1)}), bf16[512,1024]{1,0:T(8,128)(2,1)}) %all-gather.5.cloned.1.call-update) | async-done | bytes 1048592 | tf_op jit(solution)/shard_map/all_gather | solution.py:1158
  71.7 7.5 %collective-permute-done.1.x_ref = bf16[1024,1024]{1,0:T(8,128)(2,1)} collective-permute-done((bf16[1024,1024]{1,0:T(8,128)(2,1)}, bf16[1024,1024]{1,0:T(8,128)(2,1)}, u32[]{:S(2)}, u32[]{:S(2)}) %collective-permute-start.1) | collective-permute-done | bytes 2097184 | tf_op jit(solution)/shard_map/ppermute | solution.py:1151
  81.3 8.9 %collective-permute-done.2 = bf16[64,2816]{1,0:T(8,128)(2,1)S(1)} collective-permute-done((bf16[64,2816]{1,0:T(8,128)(2,1)}, bf16[64,2816]{1,0:T(8,128)(2,1)S(1)}, u32[]{:S(2)}, u32[]{:S(2)}) %collective-permute-start.2) | collective-permute-done | bytes 360480 | tf_op jit(solution)/shard_map/ppermute | solution.py:1151
  91.7 4.8 collective-permute-done.3
  96.7 8.4 %project_qkv.3 = (bf16[2048,1024]{1,0:T(8,128)(2,1)}, bf16[2048,512]{1,0:T(8,128)(2,1)}, bf16[2048,512]{1,0:T(8,128)(2,1)}, bf16[2048,512]{1,0:T(8,128)(2,1)}) custom-call(s32[1]{0:T(128)} %bitcast.3.base_ref, bf16[1024,1024]{1,0:T(8,128)(2,1)} %collective-permute-done.1.x_ref, ...), custom_call_target="tpu_custom_call", output_to_operand_aliasing={{0}: (7, {}), {1}: (8, {}), {2}: (9, {}), {3}: (10, {})} | custom-call | flops 3221225472 | bytes 10000000 | tf_op jit(solution)/shard_map/project_qkv/pallas_call | solution.py:427
  105.5 12.9 %attend_pair.4 = (bf16[2048,512]{1,0:T(8,128)(2,1)}, f32[2048,512]{1,0:T(8,128)}) custom-call(s32[1]{0:T(128)} %copy.78.len_ref, bf16[2048,512]{1,0:T(8,128)(2,1)} %get-tuple-element.168.q_ref, bf16[2048,512]{1,0:T(8,128)(2,1)} %get-tuple-element.169.k_ref, bf16[2048,512]{1,0:T(8,128)(2,1)} %get-tuple-element.170.v_ref), custom_call_target="tpu_custom_call" | custom-call | flops 4294967296 | bytes 3000000 | tf_op jit(solution)/shard_map/attend_pair/pallas_call | solution.py:508
  118.4 13.3 %attend_pair.5 = (bf16[2048,512]{1,0:T(8,128)(2,1)}, f32[2048,512]{1,0:T(8,128)}) custom-call(s32[1]{0:T(128)} %copy.78.len_ref, bf16[2048,512]{1,0:T(8,128)(2,1)} %get-tuple-element.168.q_ref, bf16[2048,512]{1,0:T(8,128)(2,1)} %get-tuple-element.169.k_ref, ...), custom_call_target="tpu_custom_call", output_to_operand_aliasing={{0}: (4, {}), {1}: (5, {})} | custom-call | flops 4294967296 | bytes 3000000 | tf_op jit(solution)/shard_map/attend_pair/pallas_call | solution.py:508
  131.7 13.1 %attend_pair.6 = (bf16[2048,512]{1,0:T(8,128)(2,1)}, f32[2048,512]{1,0:T(8,128)}) custom-call(s32[1]{0:T(128)} %copy.78.len_ref, bf16[2048,512]{1,0:T(8,128)(2,1)} %get-tuple-element.168.q_ref, bf16[2048,512]{1,0:T(8,128)(2,1)} %get-tuple-element.169.k_ref, ...), custom_call_target="tpu_custom_call", output_to_operand_aliasing={{0}: (4, {}), {1}: (5, {})} | custom-call | flops 4294967296 | bytes 3000000 | tf_op jit(solution)/shard_map/attend_pair/pallas_call | solution.py:508
  146.3 19.4 %all-gather.7.cloned.1.call-done.wgu_ref = bf16[1024,2816]{1,0:T(8,128)(2,1)} async-done(((bf16[64,2816]{1,0:T(8,128)(2,1)}), bf16[1024,2816]{1,0:T(8,128)(2,1)}) %all-gather.7.cloned.1.call-update) | async-done | bytes 5767184 | tf_op jit(solution)/shard_map/all_gather | solution.py:1158
  167.4 13.2 %attend_pair.7 = (bf16[2048,512]{1,0:T(8,128)(2,1)}, f32[2048,512]{1,0:T(8,128)}) custom-call(s32[1]{0:T(128)} %copy.78.len_ref, bf16[2048,512]{1,0:T(8,128)(2,1)} %get-tuple-element.168.q_ref, bf16[2048,512]{1,0:T(8,128)(2,1)} %get-tuple-element.169.k_ref, ...), custom_call_target="tpu_custom_call", output_to_operand_aliasing={{0}: (4, {}), {1}: (5, {})} | custom-call | flops 4294967296 | bytes 3000000 | tf_op jit(solution)/shard_map/attend_pair/pallas_call | solution.py:508
  184.1 7.2 %collective-permute-done.6.refs_1_ = bf16[1024,128]{1,0:T(8,128)(2,1)S(1)} collective-permute-done((bf16[1024,128]{1,0:T(8,128)(2,1)S(1)}, bf16[1024,128]{1,0:T(8,128)(2,1)S(1)}, u32[]{:S(2)}, u32[]{:S(2)}) %collective-permute-start.6) | collective-permute-done | bytes 262176 | tf_op jit(solution)/shard_map/ppermute | solution.py:1151
  192.0 8.2 %resid_rows.1 = (f32[1024,1024]{1,0:T(8,128)}, bf16[1024,1024]{1,0:T(8,128)(2,1)}, bf16[1024,1024]{1,0:T(8,128)(2,1)}) custom-call(s32[1]{0:T(128)} %bitcast.base_ref, bf16[1024,1024]{1,0:T(8,128)(2,1)} %x_ref.5, f32[1,1024]{1,0:T(1,128)} %get-tuple-element.306.gain_ref, bf16[512,1024]{1,0:T(8,128)(2,1)} %convert_element_type.139.w_own_ref, ...), custom_call_target="tpu_custom_call" | custom-call | flops 2147483648 | bytes 14000000 | tf_op jit(solution)/shard_map/resid_rows/pallas_call | solution.py:659
  200.1 35.9 %swiglu_half.2 = (bf16[1024,1024]{1,0:T(8,128)(2,1)}, bf16[1024,1024]{1,0:T(8,128)(2,1)}, bf16[512,4224]{1,0:T(8,128)(2,1)}, bf16[512,4224]{1,0:T(8,128)(2,1)}) custom-call(s32[2]{0:T(128)} %pad_add_fusion.place_ref, bf16[1024,1024]{1,0:T(8,128)(2,1)} %get-tuple-element.190.n_ref, bf16[1024,1024]{1,0:T(8,128)(2,1)} %broadcast_select_fusion.dy_ref, ...), custom_call_target="tpu_custom_call" | custom-call | flops 26575110144 | bytes 36000000 | tf_op jit(solution)/shard_map/swiglu_half/pallas_call | solution.py:781
  236.2 35.9 %swiglu_half.3 = (bf16[1024,1024]{1,0:T(8,128)(2,1)}, bf16[1024,1024]{1,0:T(8,128)(2,1)}, bf16[512,5376]{1,0:T(8,128)(2,1)}, bf16[512,5376]{1,0:T(8,128)(2,1)}) custom-call(s32[2]{0:T(128)} %pad_add_fusion.place_ref, bf16[1024,1024]{1,0:T(8,128)(2,1)} %get-tuple-element.190.n_ref, bf16[1024,1024]{1,0:T(8,128)(2,1)} %broadcast_select_fusion.dy_ref, ...), custom_call_target="tpu_custom_call" | custom-call | flops 26575110144 | bytes 36000000 | tf_op jit(solution)/shard_map/swiglu_half/pallas_call | solution.py:781
  272.1 4.1 add_convert_fusion.3
  276.2 12.6 %after_rows.1 = (bf16[1024,1024]{1,0:T(8,128)(2,1)}, f32[1024,1024]{1,0:T(8,128)}, bf16[1024,1024]{1,0:T(8,128)(2,1)}, bf16[1024,512]{1,0:T(8,128)(2,1)}, bf16[1024,512]{1,0:T(8,128)(2,1)}, /*index=5*/f32[1,1024]{1,0:T(1,128)}) custom-call(f32[1024,1024]{1,0:T(8,128)} %get-tuple-element.181.h_ref, bf16[1024,1024]{1,0:T(8,128)(2,1)} %get-tuple-element.186.y1_ref, ...), custom_call_target="tpu_custom_call" | custom-call | flops 2147483648 | bytes 36000000 | tf_op jit(solution)/shard_map/after_rows/pallas_call | solution.py:909
  288.8 7.6 %grad_out.1 = (bf16[512,5376]{1,0:T(8,128)(2,1)}, bf16[512,5376]{1,0:T(8,128)(2,1)}) custom-call(s32[2]{0:T(128)} %pad_add_fusion.place_ref, bf16[1024,1024]{1,0:T(8,128)(2,1)} %get-tuple-element.208.dhb_ref, bf16[1024,1024]{1,0:T(8,128)(2,1)} %get-tuple-element.209.o_ref, ...), custom_call_target="tpu_custom_call", output_to_operand_aliasing={{0}: (3, {}), {1}: (4, {})} | custom-call | flops 2147483648 | bytes 7000000 | tf_op jit(solution)/shard_map/grad_out/pallas_call | solution.py:815
  299.9 22.2 %collective-permute-done.8 = bf16[1024,128]{1,0:T(8,128)(2,1)S(1)} collective-permute-done((bf16[1024,128]{1,0:T(8,128)(2,1)S(1)}, bf16[1024,128]{1,0:T(8,128)(2,1)S(1)}, u32[]{:S(2)}, u32[]{:S(2)}) %collective-permute-start.8) | collective-permute-done | bytes 262176 | tf_op jit(solution)/shard_map/ppermute | solution.py:1151
  323.1 26.2 %attend_back_pair.4 = (f32[2048,512]{1,0:T(8,128)}, bf16[2048,1536]{1,0:T(8,128)(2,1)}, bf16[1024,384]{1,0:T(8,128)(2,1)}) custom-call(s32[2]{0:T(128)} %pad_add_fusion.1.len_ref, bf16[2048,512]{1,0:T(8,128)(2,1)} %get-tuple-element.168.q_ref, bf16[2048,512]{1,0:T(8,128)(2,1)} %get-tuple-element.169.k_ref, bf16[2048,512]{1,0:T(8,128)(2,1)} %get-tuple-element.170.v_ref, ...), custom_call_target="tpu_custom_call" | custom-call | flops 10737418240 | bytes 6000000 | tf_op jit(solution)/shard_map/attend_back_pair/pallas_call | solution.py:614
  350.8 4.8 add_convert_fusion
  357.8 26.6 %attend_back_pair.5 = (f32[2048,512]{1,0:T(8,128)}, bf16[2048,1536]{1,0:T(8,128)(2,1)}, bf16[1024,384]{1,0:T(8,128)(2,1)}) custom-call(s32[2]{0:T(128)} %pad_add_fusion.1.len_ref, bf16[2048,512]{1,0:T(8,128)(2,1)} %get-tuple-element.168.q_ref, bf16[2048,512]{1,0:T(8,128)(2,1)} %get-tuple-element.169.k_ref, ...), custom_call_target="tpu_custom_call", output_to_operand_aliasing={{0}: (9, {}), {1}: (10, {})} | custom-call | flops 10737418240 | bytes 6000000 | tf_op jit(solution)/shard_map/attend_back_pair/pallas_call | solution.py:614
  396.6 26.5 %attend_back_pair.6 = (f32[2048,512]{1,0:T(8,128)}, bf16[2048,1536]{1,0:T(8,128)(2,1)}, bf16[1024,384]{1,0:T(8,128)(2,1)}) custom-call(s32[2]{0:T(128)} %pad_add_fusion.1.len_ref, bf16[2048,512]{1,0:T(8,128)(2,1)} %get-tuple-element.168.q_ref, bf16[2048,512]{1,0:T(8,128)(2,1)} %get-tuple-element.169.k_ref, ...), custom_call_target="tpu_custom_call", output_to_operand_aliasing={{0}: (9, {}), {1}: (10, {})} | custom-call | flops 10737418240 | bytes 6000000 | tf_op jit(solution)/shard_map/attend_back_pair/pallas_call | solution.py:614
  432.7 26.4 %attend_back_pair.7 = (f32[2048,512]{1,0:T(8,128)}, bf16[2048,1536]{1,0:T(8,128)(2,1)}, bf16[1024,384]{1,0:T(8,128)(2,1)}) custom-call(s32[2]{0:T(128)} %pad_add_fusion.1.len_ref, bf16[2048,512]{1,0:T(8,128)(2,1)} %get-tuple-element.168.q_ref, bf16[2048,512]{1,0:T(8,128)(2,1)} %get-tuple-element.169.k_ref, ...), custom_call_target="tpu_custom_call", output_to_operand_aliasing={{0}: (9, {}), {1}: (10, {})} | custom-call | flops 10737418240 | bytes 6000000 | tf_op jit(solution)/shard_map/attend_back_pair/pallas_call | solution.py:614
  459.2 15.1 %grad_qkv.1 = (bf16[512,1536]{1,0:T(8,128)(2,1)}, bf16[512,1536]{1,0:T(8,128)(2,1)}, f32[1024,128]{1,0:T(8,128)}) custom-call(s32[2]{0:T(128)} %pad_add_fusion.place_ref, bf16[2048,1024]{1,0:T(8,128)(2,1)} %get-tuple-element.202.n_ref, bf16[2048,1536]{1,0:T(8,128)(2,1)} %get-tuple-element.234.dqkv_ref.refs_0_, ...), custom_call_target="tpu_custom_call" | custom-call | flops 6442450944 | bytes 14000000 | tf_op jit(solution)/shard_map/grad_qkv/pallas_call | solution.py:858
  485.6 12.0 %collective-permute-done.23.refs_4_ = bf16[1024,384]{1,0:T(8,128)(2,1)S(1)} collective-permute-done((bf16[1024,384]{1,0:T(8,128)(2,1)}, bf16[1024,384]{1,0:T(8,128)(2,1)S(1)}, u32[]{:S(2)}, u32[]{:S(2)}) %collective-permute-start.23) | collective-permute-done | bytes 786464 | tf_op jit(solution)/shard_map/ppermute | solution.py:1151
  499.2 13.6 %input_rows.1 = f32[1024,1024]{1,0:T(8,128)} custom-call(s32[1]{0:T(128)} %bitcast.base_ref, bf16[1024,1024]{1,0:T(8,128)(2,1)} %x_ref.5, f32[1024,1024]{1,0:T(8,128)} %get-tuple-element.243.dh_ref, f32[1,1024]{1,0:T(1,128)} %get-tuple-element.305.gain_ref, bf16[3,1024,512]{2,1,0:T(8,128)(2,1)} %bitcast_convert_fusion.w_ref.w_own_ref, ...), custom_call_target="tpu_custom_call" | custom-call | flops 6442450944 | bytes 20000000 | tf_op jit(solution)/shard_map/input_rows/pallas_call | solution.py:948
  512.8 29.6 %collective-permute-done.27 = bf16[64,5376]{1,0:T(8,128)(2,1)} collective-permute-done((bf16[64,5376]{1,0:T(8,128)(2,1)}, bf16[64,5376]{1,0:T(8,128)(2,1)}, u32[]{:S(2)}, u32[]{:S(2)}) %collective-permute-start.27) | collective-permute-done | bytes 688160 | tf_op jit(solution)/shard_map/ppermute | solution.py:1083
  552.0 10.5 %collective-permute-done.35 = bf16[64,4736]{1,0:T(8,128)(2,1)S(1)} collective-permute-done((bf16[64,4736]{1,0:T(8,128)(2,1)S(1)}, bf16[64,4736]{1,0:T(8,128)(2,1)S(1)}, u32[]{:S(2)}, u32[]{:S(2)}) %collective-permute-start.35) | collective-permute-done | bytes 606240 | tf_op jit(solution)/shard_map/ppermute | solution.py:1151
  567.4 6.9 %step_mlp.1 = (f32[64,2,1408]{2,1,0:T(2,128)}, f32[64,2,1408]{2,1,0:T(2,128)}, f32[64,2,1408]{2,1,0:T(2,128)}, f32[64,2,1408]{2,1,0:T(2,128)}, f32[64,1408]{1,0:...) custom-call(s32[3]{0:T(128)} %pad_add_fusion.2.place_ref, ...), custom_call_target="tpu_custom_call" | custom-call | bytes 14000000 | tf_op jit(solution)/shard_map/step_mlp/pallas_call | solution.py:995
  (169 shorter events, 93.0 us)
Async XLA Ops:
  7.2 64.5 %all-gather.5.cloned.1.call-start = ((), (), s32[]{:S(2)}) async-start(), calls=%async_computation | async-start | bytes 1114112 | tf_op jit(solution)/shard_map/all_gather | solution.py:1158
  8.2 23.7 %collective-permute-start = (bf16[32,1024]{1,0:T(8,128)(2,1)S(1)}, bf16[32,1024]{1,0:T(8,128)(2,1)S(1)}, u32[]{:S(2)}, u32[]{:S(2)}) collective-permute-start(bf16[32,1024]{1,0:T(8,128)(2,1)S(1)} %dynamic-slice_convert_fusion.9), channel_id=1, source_target_pairs={{0,1},{1,0},{2,3},{3,2},{4,5},{5,4},{6,7},{7,6},{8,9},{9,8},{10,11... | collective-permute-start | bytes 196616 | tf_op jit(solution)/shard_map/ppermute | solution.py:1151
  31.8 47.4 %collective-permute-start.1 = (bf16[1024,1024]{1,0:T(8,128)(2,1)}, bf16[1024,1024]{1,0:T(8,128)(2,1)}, u32[]{:S(2)}, u32[]{:S(2)}) collective-permute-start(bf16[1024,1024]{1,0:T(8,128)(2,1)} %x_ref.5), channel_id=1, source_target_pairs={{0,1},{1,0},{2,3},{3,2},{4,5},{5,4},{6,7},{7,6},{8,9},{9,8},{10,11... | collective-permute-start | bytes 6291464 | tf_op jit(solution)/shard_map/ppermute | solution.py:1151
  32.5 133.2 %all-gather.7.cloned.1.call-start = ((), (), s32[]{:S(2)}) async-start(), calls=%async_computation.1 | async-start | bytes 6127616 | tf_op jit(solution)/shard_map/all_gather | solution.py:1158
  105.2 130.9 %all-gather.9.cloned.1.call-start = ((), (), s32[]{:S(2)}) async-start(), calls=%async_computation.2 | async-start | bytes 3063808 | tf_op jit(solution)/shard_map/all_gather | solution.py:1158
  165.8 156.4 %all-gather.11.cloned.1.call-start = ((), (), s32[]{:S(2)}) async-start(), calls=%async_computation.3 | async-start | bytes 3342336 | tf_op jit(solution)/shard_map/all_gather | solution.py:1158
  165.9 25.4 %collective-permute-start.5 = (bf16[1024,384]{1,0:T(8,128)(2,1)S(1)}, bf16[1024,384]{1,0:T(8,128)(2,1)}, u32[]{:S(2)}, u32[]{:S(2)}) collective-permute-start(bf16[1024,384]{1,0:T(8,128)(2,1)S(1)} %constant_dynamic-slice_fusion.3), channel_id=1, source_target_pairs={{0,1},{1,0},{2,3},{3,2},{4,5},{5,4},{6,7},{7,6},{8,9},{9,8},{10,11... | collective-permute-start | bytes 2359304 | tf_op jit(solution)/shard_map/ppermute | solution.py:1151
  236.0 36.1 %collective-permute-start.7 = (bf16[512,4224]{1,0:T(8,128)(2,1)}, bf16[512,4224]{1,0:T(8,128)(2,1)}, u32[]{:S(2)}, u32[]{:S(2)}) collective-permute-start(bf16[512,4224]{1,0:T(8,128)(2,1)} %get-tuple-element.195), channel_id=1, source_target_pairs={{0,2},{2,0},{4,6},{6,4},{8,10},{10,8},{12,14},{14,12},{16,18},{18,... | collective-permute-start | bytes 12976136 | tf_op jit(solution)/shard_map/ppermute | solution.py:1083
  296.4 52.9 %collective-permute-start.10 = (bf16[512,5376]{1,0:T(8,128)(2,1)}, bf16[512,5376]{1,0:T(8,128)(2,1)}, u32[]{:S(2)}, u32[]{:S(2)}) collective-permute-start(bf16[512,5376]{1,0:T(8,128)(2,1)} %get-tuple-element.213), channel_id=1, source_target_pairs={{0,2},{2,0},{4,6},{6,4},{8,10},{10,8},{12,14},{14,12},{16,18},{18,... | collective-permute-start | bytes 16515080 | tf_op jit(solution)/shard_map/ppermute | solution.py:1083
  297.0 25.2 %collective-permute-start.9 = (bf16[1024,384]{1,0:T(8,128)(2,1)S(1)}, bf16[1024,384]{1,0:T(8,128)(2,1)S(1)}, u32[]{:S(2)}, u32[]{:S(2)}) collective-permute-start(bf16[1024,384]{1,0:T(8,128)(2,1)S(1)} %slice.97), channel_id=1, source_target_pairs={{0,1},{1,0},{2,3},{3,2},{4,5},{5,4},{6,7},{7,6},{8,9},{9,8},{10,11... | collective-permute-start | bytes 2359304 | tf_op jit(solution)/shard_map/ppermute | solution.py:1151
  298.5 23.7 %collective-permute-start.8 = (bf16[1024,128]{1,0:T(8,128)(2,1)S(1)}, bf16[1024,128]{1,0:T(8,128)(2,1)S(1)}, u32[]{:S(2)}, u32[]{:S(2)}) collective-permute-start(bf16[1024,128]{1,0:T(8,128)(2,1)S(1)} %slice.96), channel_id=1, source_target_pairs={{0,1},{1,0},{2,3},{3,2},{4,5},{5,4},{6,7},{7,6},{8,9},{9,8},{10,11... | collective-permute-start | bytes 786440 | tf_op jit(solution)/shard_map/ppermute | solution.py:1151
  299.8 84.6 %collective-permute-start.12 = (bf16[256,4224]{1,0:T(8,128)(2,1)}, bf16[256,4224]{1,0:T(8,128)(2,1)}, u32[]{:S(2)}, u32[]{:S(2)}) collective-permute-start(bf16[256,4224]{1,0:T(8,128)(2,1)} %add_convert_fusion.3), channel_id=1, source_target_pairs={{0,4},{2,6},{4,0},{6,2},{8,12},{10,14},{12,8},{14,10},{16,20},{18,... | collective-permute-start | bytes 6488072 | tf_op jit(solution)/shard_map/ppermute | solution.py:1083
  349.4 45.8 %collective-permute-start.13 = (bf16[1024,384]{1,0:T(8,128)(2,1)}, bf16[1024,384]{1,0:T(8,128)(2,1)}, u32[]{:S(2)}, u32[]{:S(2)}) collective-permute-start(bf16[1024,384]{1,0:T(8,128)(2,1)} %get-tuple-element.224), channel_id=1, source_target_pairs={{0,1},{1,0},{2,3},{3,2},{4,5},{5,4},{6,7},{7,6},{8,9},{9,8},{10,11... | collective-permute-start | bytes 2359304 | tf_op jit(solution)/shard_map/ppermute | solution.py:1151
  355.7 67.4 %collective-permute-start.11 = (bf16[256,5376]{1,0:T(8,128)(2,1)}, bf16[256,5376]{1,0:T(8,128)(2,1)S(1)}, u32[]{:S(2)}, u32[]{:S(2)}) collective-permute-start(bf16[256,5376]{1,0:T(8,128)(2,1)} %add_convert_fusion), channel_id=1, source_target_pairs={{0,4},{2,6},{4,0},{6,2},{8,12},{10,14},{12,8},{14,10},{16,20},{18,... | collective-permute-start | bytes 8257544 | tf_op jit(solution)/shard_map/ppermute | solution.py:1083
  391.3 67.8 %collective-permute-start.18 = (bf16[64,4224]{1,0:T(8,128)(2,1)}, bf16[64,4224]{1,0:T(8,128)(2,1)}, u32[]{:S(2)}, u32[]{:S(2)}) collective-permute-start(bf16[64,4224]{1,0:T(8,128)(2,1)} %get-tuple-element.288), channel_id=1, source_target_pairs={{0,24},{2,26},{4,28},{6,30},{8,0},{10,2},{12,4},{14,6},{16,8},{18,... | collective-permute-start | bytes 1622024 | tf_op jit(solution)/shard_map/ppermute | solution.py:1083
  393.3 65.8 %collective-permute-start.17 = (bf16[64,4224]{1,0:T(8,128)(2,1)}, bf16[64,4224]{1,0:T(8,128)(2,1)}, u32[]{:S(2)}, u32[]{:S(2)}) collective-permute-start(bf16[64,4224]{1,0:T(8,128)(2,1)} %get-tuple-element.289), channel_id=1, source_target_pairs={{0,16},{2,18},{4,20},{6,22},{8,24},{10,26},{12,28},{14,30},{16,0},... | collective-permute-start | bytes 1622024 | tf_op jit(solution)/shard_map/ppermute | solution.py:1083
  394.1 65.0 %collective-permute-start.16 = (bf16[64,4224]{1,0:T(8,128)(2,1)}, bf16[64,4224]{1,0:T(8,128)(2,1)}, u32[]{:S(2)}, u32[]{:S(2)}) collective-permute-start(bf16[64,4224]{1,0:T(8,128)(2,1)} %get-tuple-element.290), channel_id=1, source_target_pairs={{0,8},{2,10},{4,12},{6,14},{8,16},{10,18},{12,20},{14,22},{16,24},... | collective-permute-start | bytes 1622024 | tf_op jit(solution)/shard_map/ppermute | solution.py:1083
  395.2 36.7 %collective-permute-start.14 = (bf16[1024,384]{1,0:T(8,128)(2,1)}, bf16[1024,384]{1,0:T(8,128)(2,1)}, u32[]{:S(2)}, u32[]{:S(2)}) collective-permute-start(bf16[1024,384]{1,0:T(8,128)(2,1)} %get-tuple-element.230), channel_id=1, source_target_pairs={{0,1},{1,0},{2,3},{3,2},{4,5},{5,4},{6,7},{7,6},{8,9},{9,8},{10,11... | collective-permute-start | bytes 2359304 | tf_op jit(solution)/shard_map/ppermute | solution.py:1151
  423.1 36.1 %collective-permute-start.15 = (bf16[1024,384]{1,0:T(8,128)(2,1)}, bf16[1024,384]{1,0:T(8,128)(2,1)}, u32[]{:S(2)}, u32[]{:S(2)}) collective-permute-start(bf16[1024,384]{1,0:T(8,128)(2,1)} %get-tuple-element.233), channel_id=1, source_target_pairs={{0,1},{1,0},{2,3},{3,2},{4,5},{5,4},{6,7},{7,6},{8,9},{9,8},{10,11... | collective-permute-start | bytes 2359304 | tf_op jit(solution)/shard_map/ppermute | solution.py:1151
  477.8 19.9 %collective-permute-start.23 = (bf16[1024,384]{1,0:T(8,128)(2,1)}, bf16[1024,384]{1,0:T(8,128)(2,1)S(1)}, u32[]{:S(2)}, u32[]{:S(2)}) collective-permute-start(bf16[1024,384]{1,0:T(8,128)(2,1)} %get-tuple-element.248), channel_id=1, source_target_pairs={{0,1},{1,0},{2,3},{3,2},{4,5},{5,4},{6,7},{7,6},{8,9},{9,8},{10,11... | collective-permute-start | bytes 2359304 | tf_op jit(solution)/shard_map/ppermute | solution.py:1151
  479.0 33.7 %collective-permute-start.28 = (bf16[64,5376]{1,0:T(8,128)(2,1)}, bf16[64,5376]{1,0:T(8,128)(2,1)}, u32[]{:S(2)}, u32[]{:S(2)}) collective-permute-start(bf16[64,5376]{1,0:T(8,128)(2,1)} %get-tuple-element.285), channel_id=1, source_target_pairs={{0,24},{2,26},{4,28},{6,30},{8,0},{10,2},{12,4},{14,6},{16,8},{18,... | collective-permute-start | bytes 2064392 | tf_op jit(solution)/shard_map/ppermute | solution.py:1083
  481.8 60.5 %collective-permute-start.27 = (bf16[64,5376]{1,0:T(8,128)(2,1)}, bf16[64,5376]{1,0:T(8,128)(2,1)}, u32[]{:S(2)}, u32[]{:S(2)}) collective-permute-start(bf16[64,5376]{1,0:T(8,128)(2,1)} %get-tuple-element.286), channel_id=1, source_target_pairs={{0,16},{2,18},{4,20},{6,22},{8,24},{10,26},{12,28},{14,30},{16,0},... | collective-permute-start | bytes 2064392 | tf_op jit(solution)/shard_map/ppermute | solution.py:1083
  482.1 60.2 %collective-permute-start.26 = (bf16[64,5376]{1,0:T(8,128)(2,1)}, bf16[64,5376]{1,0:T(8,128)(2,1)}, u32[]{:S(2)}, u32[]{:S(2)}) collective-permute-start(bf16[64,5376]{1,0:T(8,128)(2,1)} %get-tuple-element.287), channel_id=1, source_target_pairs={{0,8},{2,10},{4,12},{6,14},{8,16},{10,18},{12,20},{14,22},{16,24},... | collective-permute-start | bytes 2064392 | tf_op jit(solution)/shard_map/ppermute | solution.py:1083
  483.8 58.5 %collective-permute-start.24 = (bf16[256,1536]{1,0:T(8,128)(2,1)S(1)}, bf16[256,1536]{1,0:T(8,128)(2,1)S(1)}, u32[]{:S(2)}, u32[]{:S(2)}) collective-permute-start(bf16[256,1536]{1,0:T(8,128)(2,1)S(1)} %add_convert_fusion.5), channel_id=1, source_target_pairs={{0,4},{2,6},{4,0},{6,2},{8,12},{10,14},{12,8},{14,10},{16,20},{18,... | collective-permute-start | bytes 2359304 | tf_op jit(solution)/shard_map/ppermute | solution.py:1083
  497.7 44.7 %collective-permute-start.25 = (f32[2,1024]{1,0:T(2,128)S(1)}, f32[2,1024]{1,0:T(2,128)S(1)}, u32[]{:S(2)}, u32[]{:S(2)}) collective-permute-start(f32[2,1024]{1,0:T(2,128)S(1)} %add_add_fusion), channel_id=1, source_target_pairs={{0,4},{2,6},{4,0},{6,2},{8,12},{10,14},{12,8},{14,10},{16,20},{18,... | collective-permute-start | bytes 24584 | tf_op jit(solution)/shard_map/ppermute | solution.py:1083
  542.4 9.7 %collective-permute-start.34 = (f32[2,1024]{1,0:T(2,128)S(1)}, f32[2,1024]{1,0:T(2,128)S(1)}, u32[]{:S(2)}, u32[]{:S(2)}) collective-permute-start(f32[2,1024]{1,0:T(2,128)S(1)} %add.187), channel_id=1, source_target_pairs={{0,24},{2,26},{4,28},{6,30},{8,0},{10,2},{12,4},{14,6},{16,8},{18,... | collective-permute-start | bytes 24584 | tf_op jit(solution)/shard_map/ppermute | solution.py:1083
  542.4 31.8 %collective-permute-start.33 = (f32[2,1024]{1,0:T(2,128)S(1)}, f32[2,1024]{1,0:T(2,128)S(1)}, u32[]{:S(2)}, u32[]{:S(2)}) collective-permute-start(f32[2,1024]{1,0:T(2,128)S(1)} %add.187), channel_id=1, source_target_pairs={{0,16},{2,18},{4,20},{6,22},{8,24},{10,26},{12,28},{14,30},{16,0},... | collective-permute-start | bytes 24584 | tf_op jit(solution)/shard_map/ppermute | solution.py:1083
  544.2 30.1 %collective-permute-start.32 = (f32[2,1024]{1,0:T(2,128)S(1)}, f32[2,1024]{1,0:T(2,128)S(1)}, u32[]{:S(2)}, u32[]{:S(2)}) collective-permute-start(f32[2,1024]{1,0:T(2,128)S(1)} %add.187), channel_id=1, source_target_pairs={{0,8},{2,10},{4,12},{6,14},{8,16},{10,18},{12,20},{14,22},{16,24},... | collective-permute-start | bytes 24584 | tf_op jit(solution)/shard_map/ppermute | solution.py:1083
  548.4 14.1 %collective-permute-start.35 = (bf16[64,4736]{1,0:T(8,128)(2,1)S(1)}, bf16[64,4736]{1,0:T(8,128)(2,1)S(1)}, u32[]{:S(2)}, u32[]{:S(2)}) collective-permute-start(bf16[64,4736]{1,0:T(8,128)(2,1)S(1)} %slice.144), channel_id=1, source_target_pairs={{0,1},{1,0},{2,3},{3,2},{4,5},{5,4},{6,7},{7,6},{8,9},{9,8},{10,11... | collective-permute-start | bytes 1818632 | tf_op jit(solution)/shard_map/ppermute | solution.py:1151
  550.1 24.1 %collective-permute-start.31 = (bf16[64,1536]{1,0:T(8,128)(2,1)S(1)}, bf16[64,1536]{1,0:T(8,128)(2,1)S(1)}, u32[]{:S(2)}, u32[]{:S(2)}) collective-permute-start(bf16[64,1536]{1,0:T(8,128)(2,1)S(1)} %get-tuple-element.291), channel_id=1, source_target_pairs={{0,24},{2,26},{4,28},{6,30},{8,0},{10,2},{12,4},{14,6},{16,8},{18,... | collective-permute-start | bytes 589832 | tf_op jit(solution)/shard_map/ppermute | solution.py:1083
  552.0 22.2 %collective-permute-start.30 = (bf16[64,1536]{1,0:T(8,128)(2,1)S(1)}, bf16[64,1536]{1,0:T(8,128)(2,1)S(1)}, u32[]{:S(2)}, u32[]{:S(2)}) collective-permute-start(bf16[64,1536]{1,0:T(8,128)(2,1)S(1)} %get-tuple-element.292), channel_id=1, source_target_pairs={{0,16},{2,18},{4,20},{6,22},{8,24},{10,26},{12,28},{14,30},{16,0},... | collective-permute-start | bytes 589832 | tf_op jit(solution)/shard_map/ppermute | solution.py:1083
  562.6 11.7 %collective-permute-start.29 = (bf16[64,1536]{1,0:T(8,128)(2,1)S(1)}, bf16[64,1536]{1,0:T(8,128)(2,1)S(1)}, u32[]{:S(2)}, u32[]{:S(2)}) collective-permute-start(bf16[64,1536]{1,0:T(8,128)(2,1)S(1)} %get-tuple-element.293), channel_id=1, source_target_pairs={{0,8},{2,10},{4,12},{6,14},{8,16},{10,18},{12,20},{14,22},{16,24},... | collective-permute-start | bytes 589832 | tf_op jit(solution)/shard_map/ppermute | solution.py:1083
  (30 other events, 326.8 us)
Sparse Core Ops, SparseCore 0:
  32.6 39.0 all-gather.4
  105.3 60.3 all-gather.6
  168.6 43.0 all-gather.8
  236.3 43.7 all-gather.10
